TPU v7x, 256 devices: a whole 4x4x8 slice. The times are simulated.
256 devices in a mesh: view: 32 (over z, y), mp: 8 (over x, core).
Axes of the slice: x: 4, y: 4, z: 8, core: 2. Of those that a mesh axis runs over, the one named last changes fastest.
Arguments:
- tokens: bfloat16 [128, 384, 1024], P('view', None, 'mp'), may hold values from -6 to 6
- pairs: int32 [512, 2], P('view'), may hold values from 0 to 127, as said below
- w_embed: bfloat16 [1024, 768], replicated, may hold values from -0.1875 to 0.1875
- w_query: bfloat16 [2, 768, 768], replicated, may hold values from -8 to 8
- w_keyval: bfloat16 [2, 768, 1536], replicated, may hold values from -0.21875 to 0.21875
- w_out: bfloat16 [2, 768, 768], replicated, may hold values from -0.21875 to 0.21875
- w_head: bfloat16 [2, 4, 768], replicated, may hold values from -0.21875 to 0.21875
- gains: float32 [2, 3, 768], replicated, may hold values from 0.1 to 1.9
Outputs:
- view_sums: float32 [128, 4, 384], P('view')
Inputs may be any that keep to these rules, and one draw needn't show every extreme that they name: Owner of a view: view // 4. Among the 32 sides of the pairs of one index of view, at most 2 name views of one owner, and in every such block some owner is named exactly 2 times. The two views of a pair differ.
All inputs are finite; a program needn't handle non-finite values.
Results may differ from a plain program's by a relative error of at most 0.012.
Values may be sent and summed in bfloat16 or wider, within the bound.
A program may use at most 128 MiB of HBM per device.

v0:
```python
import jax
import jax.numpy as jnp
from jax import lax
from jax.sharding import PartitionSpec as P

HEADS = 12


def layer_norm(values):
    mean = jnp.mean(values, axis=-1, keepdims=True)
    centred = values - mean
    var = jnp.mean(centred * centred, axis=-1, keepdims=True)
    return centred * lax.rsqrt(var + 1e-06)


def decode_sides(emb, w_query, w_keyval, w_out, w_head, gains):
    width = emb.shape[-1]
    head_size = width // HEADS
    count = emb.shape[0]
    tokv = emb.shape[2]
    records = []
    for side in range(2):
        other = 1 - side
        query_in = (layer_norm(emb[:, side].astype(jnp.float32)) * gains[side, 0]).astype(
            jnp.bfloat16
        )
        memory_in = (layer_norm(emb[:, other].astype(jnp.float32)) * gains[side, 1]).astype(
            jnp.bfloat16
        )
        query = jnp.einsum(
            "ptd,de->pte", query_in, w_query[side], preferred_element_type=jnp.float32
        ).astype(jnp.bfloat16)
        keyval = jnp.einsum(
            "ptd,de->pte", memory_in, w_keyval[side], preferred_element_type=jnp.float32
        ).astype(jnp.bfloat16)
        query_h = query.reshape(count, tokv, HEADS, head_size)
        key_h = keyval[..., :width].reshape(count, tokv, HEADS, head_size)
        value_h = keyval[..., width:].reshape(count, tokv, HEADS, head_size)
        scores = jnp.einsum(
            "pqhd,pkhd->phqk", query_h, key_h, preferred_element_type=jnp.float32
        ) * (1.0 / head_size**0.5)
        probs = jax.nn.softmax(scores, axis=-1).astype(jnp.bfloat16)
        context = jnp.einsum("phqk,pkhd->pqhd", probs, value_h, preferred_element_type=jnp.float32)
        context = context.astype(jnp.bfloat16).reshape(count, tokv, width)
        updated = emb[:, side].astype(jnp.float32) + jnp.einsum(
            "ptd,de->pte", context, w_out[side], preferred_element_type=jnp.float32
        )
        final = (layer_norm(updated) * gains[side, 2]).astype(jnp.bfloat16)
        head = jnp.einsum("cd,ptd->pct", w_head[side], final, preferred_element_type=jnp.float32)
        conf = 1.0 + jnp.exp(head[:, 3])
        records.append(jnp.concatenate([conf[:, None, :] * head[:, :3], conf[:, None, :]], axis=1))
    return jnp.stack(records, axis=1)


def on_device(tokens, pairs, w_embed, w_query, w_keyval, w_out, w_head, gains):
    view_count = lax.axis_size("view")
    column_count = lax.axis_size("mp")
    column_index = lax.axis_index("mp")
    view_dev = tokens.shape[0]
    tokv = tokens.shape[1]
    feat_shard = tokens.shape[2]
    width = w_embed.shape[1]
    block_pairs = pairs.shape[0]
    pair_dev = block_pairs // column_count
    side_count = 2 * block_pairs
    slot_cap = max(2, (side_count + view_count - 1) // view_count)
    slot_total = view_count * slot_cap
    side_views = pairs.reshape(side_count)
    owners = side_views // view_dev
    local_ids = side_views % view_dev
    positions = jnp.arange(side_count, dtype=jnp.int32)
    same_owner = owners[:, None] == owners[None, :]
    slot_rank = jnp.sum(
        jnp.logical_and(same_owner, positions[None, :] < positions[:, None]), axis=1
    )
    slot_index = owners * slot_cap + slot_rank
    slot_match = jnp.arange(slot_total, dtype=jnp.int32)[:, None] == slot_index[None, :]
    wanted = jnp.sum(jnp.where(slot_match, local_ids[None, :], 0), axis=1)
    wanted = jnp.where(jnp.any(slot_match, axis=1), wanted, -1).reshape(view_count, slot_cap)
    asked = lax.all_to_all(wanted, "view", split_axis=0, concat_axis=0, tiled=True)
    picker = (asked[:, :, None] == jnp.arange(view_dev, dtype=jnp.int32)[None, None, :]).astype(
        jnp.bfloat16
    )
    payload = jnp.einsum(
        "rcv,vte->rcte", picker, tokens, preferred_element_type=jnp.float32
    ).astype(jnp.bfloat16)
    fetched = lax.all_to_all(payload, "view", split_axis=0, concat_axis=0, tiled=True)
    side_rows = jnp.take(fetched.reshape(slot_total, tokv, feat_shard), slot_index, axis=0)
    parcel = side_rows.reshape(column_count, pair_dev, 2, tokv, feat_shard)
    arrived = lax.all_to_all(parcel, "mp", split_axis=0, concat_axis=4, tiled=True)
    items = arrived.shape[1]
    full_feat = arrived.shape[4]
    emb = jnp.dot(
        arrived.reshape(items * 2 * tokv, full_feat), w_embed, preferred_element_type=jnp.float32
    )
    emb = emb.astype(jnp.bfloat16).reshape(items, 2, tokv, width)
    results = decode_sides(emb, w_query, w_keyval, w_out, w_head, gains)
    my_pairs = lax.dynamic_slice_in_dim(pairs, column_index * pair_dev, pair_dev, 0).reshape(
        2 * pair_dev
    )
    all_views = view_dev * view_count
    one_hot = (my_pairs[:, None] == jnp.arange(all_views, dtype=jnp.int32)[None, :]).astype(
        jnp.float32
    )
    flat_results = results.reshape(2 * pair_dev, 4 * tokv)
    spread = jnp.dot(one_hot.T, flat_results, precision=lax.Precision.HIGHEST).reshape(
        all_views, 4, tokv
    )
    owned = lax.psum_scatter(spread, "view", scatter_dimension=0, tiled=True)
    return lax.psum(owned, "mp")


def solution(mesh):
    return jax.shard_map(
        on_device,
        mesh=mesh,
        in_specs=(P("view", None, "mp"), P("view", None), P(), P(), P(), P(), P(), P()),
        out_specs=P("view", None, None),
        check_vma=False,
    )
```

profile of v0, /device:TPU:1, one launch (start us, length us, event | category | flops | bytes accessed | tf_op | source)
XLA Modules:
  0.0 473.6 jit_solution(5669005902016152880)
XLA Ops:
  8.0 20.4 %all_to_all.26 = s32[32,1,2]{2,1,0:T(1,128)S(1)} all-to-all(s32[32,1,2]{2,1,0:T(1,128)S(1)} %bitcast.194), channel_id=1, replica_groups=mesh['view'=32,'mp'=8] {'view'}, dimensions={0} | all-to-all | bytes 512 | tf_op jit(solution)/shard_map/all_to_all | solution.py:80
  28.5 3.1 convolution_convert_fusion
  31.6 5.1 %copy.111 = bf16[32,2,384,128]{3,2,1,0:T(8,128)(2,1)} copy(bf16[32,2,384,128]{3,0,2,1:T(8,128)(2,1)S(1)} %convolution_convert_fusion) | data formatting | bytes 12582912 | tf_op jit(solution)/shard_map/convert_element_type | solution.py:86
  36.7 5.0 %all-to-all-start.1 = ((bf16[32,2,384,128]{3,2,1,0:T(8,128)(2,1)}), bf16[32,2,384,128]{3,2,1,0:T(8,128)(2,1)}, u32[]{:S(2)}, u32[]{:S(2)}) async-start(bf16[32,2,384,128]{3,2,1,0:T(8,128)(2,1)} %copy.111), calls=%async_computation.1 | async-start | bytes 12582912 | tf_op jit(solution)/shard_map/all_to_all | solution.py:87
  42.4 135.3 %all-to-all-done.1 = bf16[32,2,384,128]{3,2,1,0:T(8,128)(2,1)} async-done(((bf16[32,2,384,128]{3,2,1,0:T(8,128)(2,1)}), bf16[32,2,384,128]{3,2,1,0:T(8,128)(2,1)}, u32[]{:S(2)}, u32[]{:S(2)}) %all-to-all-start.1) | async-done | bytes 6291488 | tf_op jit(solution)/shard_map/all_to_all | solution.py:87
  177.6 5.4 %gather_fusion = bf16[32,384,128]{2,1,0:T(8,128)(2,1)} fusion(bf16[64,384,128]{2,1,0:T(8,128)(2,1)} %bitcast.6, s32[1024]{0:T(1024)S(1)} %pad_clamp_fusion), kind=kCustom, calls=%fused_computation | custom fusion | bytes 6291584 | tf_op jit(solution)/shard_map/jit(_take)/gather | solution.py:88
  183.1 3.9 broadcast_select_fusion
  187.0 10.3 %all-to-all-start.2 = ((bf16[8,2,2,384,128]{4,3,2,1,0:T(8,128)(2,1)}), bf16[8,2,2,384,128]{4,3,2,1,0:T(8,128)(2,1)}, u32[]{:S(2)}, u32[]{:S(2)}) async-start(bf16[8,2,2,384,128]{4,3,2,1,0:T(8,128)(2,1)} %broadcast_select_fusion), calls=%async_computation.2 | async-start | bytes 6291456 | tf_op jit(solution)/shard_map/all_to_all | solution.py:90
  197.6 37.4 %all-to-all-done.2 = bf16[8,2,2,384,128]{4,3,2,1,0:T(8,128)(2,1)} async-done(((bf16[8,2,2,384,128]{4,3,2,1,0:T(8,128)(2,1)}), bf16[8,2,2,384,128]{4,3,2,1,0:T(8,128)(2,1)}, u32[]{:S(2)}, u32[]{:S(2)}) %all-to-all-start.2) | async-done | bytes 3145760 | tf_op jit(solution)/shard_map/all_to_all | solution.py:90
  235.0 3.9 copy.113
  238.9 2.8 convolution_convert_fusion.1
  245.5 1.4 copy.117
  246.9 4.1 convolution_convert_fusion.3
  251.2 1.4 copy.118
  252.6 1.4 copy.116
  254.0 8.4 %fusion.98 = (f32[2,12,384]{2,1,0:T(8,128)S(1)}, f32[2,12,384,384]{2,3,1,0:T(8,128)}) fusion(bf16[2,384,12,64]{1,3,2,0:T(8,128)(2,1)S(1)} %bitcast.187, bf16[2,384,12,64]{1,3,2,0:T(8,128)(2,1)} %bitcast.189), kind=kOutput, calls=%fused_computation.163 | convolution fusion | flops 463602048 | bytes 16551936 | tf_op jit(solution)/shard_map/sub | solution.py:42
  262.5 6.4 %fusion.37 = bf16[2,12,64,384]{3,2,1,0:T(8,128)(2,1)S(1)} fusion(bf16[2,384,12,64]{1,3,2,0:T(8,128)(2,1)S(1)} %bitcast.190, f32[2,12,384,384]{2,3,1,0:T(8,128)} %get-tuple-element.26, f32[2,12,384]{2,1,0:T(8,128)S(1)} %get-tuple-element.25), kind=kOutput, calls=%fused_computation.55 | convolution fusion | flops 460652544 | bytes 16551936 | tf_op jit(solution)/shard_map/phqk,pkhd->pqhd/dot_general | solution.py:43
  274.5 4.1 convolution_convert_fusion.2
  278.8 1.4 copy.123
  281.6 8.4 %fusion.96 = (f32[2,12,384]{2,1,0:T(8,128)S(1)}, f32[2,12,384,384]{2,3,1,0:T(8,128)}) fusion(bf16[2,384,12,64]{1,3,2,0:T(8,128)(2,1)S(1)} %bitcast.188, bf16[2,384,12,64]{1,3,2,0:T(8,128)(2,1)} %bitcast.191), kind=kOutput, calls=%fused_computation.161 | convolution fusion | flops 463602048 | bytes 16551936 | tf_op jit(solution)/shard_map/sub | solution.py:42
  290.1 6.4 %fusion.36 = bf16[2,12,64,384]{3,2,1,0:T(8,128)(2,1)S(1)} fusion(bf16[2,384,12,64]{1,3,2,0:T(8,128)(2,1)S(1)} %bitcast.192, f32[2,12,384,384]{2,3,1,0:T(8,128)} %get-tuple-element.22, f32[2,12,384]{2,1,0:T(8,128)S(1)} %get-tuple-element.21), kind=kOutput, calls=%fused_computation.54 | convolution fusion | flops 460652544 | bytes 16551936 | tf_op jit(solution)/shard_map/phqk,pkhd->pqhd/dot_general | solution.py:43
  298.9 1.5 fusion.88
  301.6 138.3 %all-reduce.3.cloned.1.call-done = f32[128,4,384]{2,0,1:T(8,128)} async-done(((f32[128,4,384]{2,0,1:T(8,128)}), f32[128,4,384]{2,0,1:T(8,128)}) %all-reduce.3.cloned.1.call-update) | async-done | bytes 786448
  440.7 25.4 %psum.7 = f32[4,4,384]{2,0,1:T(4,128)S(1)} all-reduce(f32[4,4,384]{2,0,1:T(4,128)S(1)} %constant_dynamic-slice_fusion), channel_id=1, replica_groups=mesh['view'=32,'mp'=8] {'mp'}, use_global_device_ids=true, to_apply=%region_16.17 | all-reduce | flops 6144 | bytes 49152 | tf_op jit(solution)/shard_map/psum | solution.py:110
  (93 shorter events, 17.7 us)
Async XLA Ops:
  6.5 232.4 %copy-start = (bf16[1024,768]{1,0:T(8,128)(2,1)S(1)}, bf16[1024,768]{1,0:T(8,128)(2,1)}, u32[]{:S(2)}) copy-start(bf16[1024,768]{1,0:T(8,128)(2,1)} %param.10) | copy-start | bytes 4718596
  36.7 5.2 %copy-start.11 = (s32[16,2]{0,1:T(2,128)S(1)}, s32[16,2]{0,1:T(2,128)}, u32[]{:S(2)}) copy-start(s32[16,2]{0,1:T(2,128)} %param.9) | copy-start | bytes 388
  36.7 140.9 %all-to-all-start.1 = ((bf16[32,2,384,128]{3,2,1,0:T(8,128)(2,1)}), bf16[32,2,384,128]{3,2,1,0:T(8,128)(2,1)}, u32[]{:S(2)}, u32[]{:S(2)}) async-start(bf16[32,2,384,128]{3,2,1,0:T(8,128)(2,1)} %copy.111), calls=%async_computation.1 | async-start | bytes 12582912 | tf_op jit(solution)/shard_map/all_to_all | solution.py:87
  187.0 10.6 %copy-start.9 = (f32[2,3,768]{2,0,1:T(2,128)S(1)}, f32[2,3,768]{2,0,1:T(2,128)}, u32[]{:S(2)}) copy-start(f32[2,3,768]{2,0,1:T(2,128)} %param.15) | copy-start | bytes 55300
  187.0 48.0 %all-to-all-start.2 = ((bf16[8,2,2,384,128]{4,3,2,1,0:T(8,128)(2,1)}), bf16[8,2,2,384,128]{4,3,2,1,0:T(8,128)(2,1)}, u32[]{:S(2)}, u32[]{:S(2)}) async-start(bf16[8,2,2,384,128]{4,3,2,1,0:T(8,128)(2,1)} %broadcast_select_fusion), calls=%async_computation.2 | async-start | bytes 6291456 | tf_op jit(solution)/shard_map/all_to_all | solution.py:90
  197.3 242.6 %all-reduce.3.cloned.1.call-start = ((), (), s32[]{:S(2)}) async-start(), calls=%async_computation.3 | async-start | bytes 1572864
  241.7 1.4 copy-start.2
  241.7 2.5 copy-start.12
  252.6 1.4 copy-start.5
  254.0 8.5 %copy-start.7 = (bf16[2,384,768]{1,2,0:T(8,128)(2,1)S(1)}, bf16[2,384,768]{1,2,0:T(8,128)(2,1)}, u32[]{:S(2)}) copy-start(bf16[2,384,768]{1,2,0:T(8,128)(2,1)} %copy.116) | copy-start | bytes 3538948
  262.5 6.4 %copy-start.3 = (bf16[1536,768]{1,0:T(8,128)(2,1)S(1)}, bf16[1536,768]{1,0:T(8,128)(2,1)}, u32[]{:S(2)}) copy-start(bf16[1536,768]{1,0:T(8,128)(2,1)} %copy-done.2) | copy-start | bytes 7077892
  262.5 6.4 %copy-start.14 = (bf16[2,768,768]{2,1,0:T(8,128)(2,1)S(1)}, bf16[2,768,768]{2,1,0:T(8,128)(2,1)}, u32[]{:S(2)}) copy-start(bf16[2,768,768]{2,1,0:T(8,128)(2,1)} %param.13) | copy-start | bytes 7077892
  270.2 0.7 copy-start.10
  270.2 1.7 copy-start.13
  280.2 1.4 copy-start.6
  281.6 8.5 %copy-start.8 = (bf16[2,384,768]{1,2,0:T(8,128)(2,1)S(1)}, bf16[2,384,768]{1,2,0:T(8,128)(2,1)}, u32[]{:S(2)}) copy-start(bf16[2,384,768]{1,2,0:T(8,128)(2,1)} %copy.121) | copy-start | bytes 3538948
  290.1 6.4 %copy-start.4 = (bf16[1536,768]{1,0:T(8,128)(2,1)S(1)}, bf16[1536,768]{1,0:T(8,128)(2,1)}, u32[]{:S(2)}) copy-start(bf16[1536,768]{1,0:T(8,128)(2,1)} %copy-done.2) | copy-start | bytes 7077892
  290.1 6.4 %copy-start.15 = (bf16[2,768,768]{2,1,0:T(8,128)(2,1)S(1)}, bf16[2,768,768]{2,1,0:T(8,128)(2,1)}, u32[]{:S(2)}) copy-start(bf16[2,768,768]{2,1,0:T(8,128)(2,1)} %param.13) | copy-start | bytes 7077892
  297.8 168.9 %copy-start.1 = (bf16[1024,768]{1,0:T(8,128)(2,1)S(1)}, bf16[1024,768]{1,0:T(8,128)(2,1)}, u32[]{:S(2)}) copy-start(bf16[1024,768]{1,0:T(8,128)(2,1)} %param.10) | copy-start | bytes 4718596
  298.2 2.2 copy-start.16
Sparse Core Ops, SparseCore 0:
  300.5 139.3 all-reduce.2
where the time goes:
time: 475 us; the launch traced here: 474 us
  waiting for transfers between devices  311 us (65%)
  matrix products  51.4 us (11%)
  blocking collectives  45.8 us (10%)
  local copies, waits for them, and re-layouts  29.2 us (6%)
  starting transfers between devices  15.3 us (3%)
  between operations  14.4 us (3%)
  other arithmetic  6.52 us (1%)
    unnamed x2, waiting for transfers between devices  138 us
    all_to_all x1, waiting for transfers between devices, on_device(): lax.all_to_all(payload, 'view', split_axis=0, concat_axis=0, tiled=True)  135 us
    all_to_all x1, waiting for transfers between devices, on_device(): lax.all_to_all(parcel, 'mp', split_axis=0, concat_axis=4, tiled=True)  37.4 us
    psum x1, blocking collectives, on_device(): return lax.psum(owned, 'mp')  25.4 us
    all_to_all x1, blocking collectives, on_device(): lax.all_to_all(wanted, 'view', split_axis=0, concat_axis=0, tiled=True)  20.4 us
    sub x2, matrix products, decode_sides(): probs = jax.nn.softmax(scores, axis=-1).astype(jnp.bfloat16)  16.9 us
    dot_general x2, matrix products, decode_sides(): jnp.einsum('phqk,pkhd->pqhd', probs, value_h, preferred_element_type=jnp....  12.8 us
    all_to_all x1, starting transfers between devices, on_device(): lax.all_to_all(parcel, 'mp', split_axis=0, concat_axis=4, tiled=True)  10.3 us
  transfers between devices with their start and end apart: 3, of which 3 were waited for; matrix products, arithmetic and copies ran while one was open for 0% of the time, Pallas kernels for 0%

commit v1 on v0

v1 whole, which is shorter than its diff:
```python
import jax
import jax.numpy as jnp
from jax import lax
from jax.experimental import pallas as pl
from jax.experimental.pallas import tpu as pltpu
from jax.sharding import PartitionSpec as P

HEADS = 12


def layer_norm(values):
    mean = jnp.mean(values, axis=-1, keepdims=True)
    centred = values - mean
    var = jnp.mean(centred * centred, axis=-1, keepdims=True)
    return centred * lax.rsqrt(var + 1e-06)


def decode_sides(emb, w_query, w_keyval, w_out, w_head, gains):
    width = emb.shape[-1]
    head_size = width // HEADS
    count = emb.shape[0]
    tokv = emb.shape[2]
    records = []
    for side in range(2):
        other = 1 - side
        query_in = (layer_norm(emb[:, side].astype(jnp.float32)) * gains[side, 0]).astype(
            jnp.bfloat16
        )
        memory_in = (layer_norm(emb[:, other].astype(jnp.float32)) * gains[side, 1]).astype(
            jnp.bfloat16
        )
        query = jnp.einsum(
            "ptd,de->pte", query_in, w_query[side], preferred_element_type=jnp.float32
        ).astype(jnp.bfloat16)
        keyval = jnp.einsum(
            "ptd,de->pte", memory_in, w_keyval[side], preferred_element_type=jnp.float32
        ).astype(jnp.bfloat16)
        query_h = query.reshape(count, tokv, HEADS, head_size)
        key_h = keyval[..., :width].reshape(count, tokv, HEADS, head_size)
        value_h = keyval[..., width:].reshape(count, tokv, HEADS, head_size)
        scores = jnp.einsum(
            "pqhd,pkhd->phqk", query_h, key_h, preferred_element_type=jnp.float32
        ) * (1.0 / head_size**0.5)
        probs = jax.nn.softmax(scores, axis=-1).astype(jnp.bfloat16)
        context = jnp.einsum("phqk,pkhd->pqhd", probs, value_h, preferred_element_type=jnp.float32)
        context = context.astype(jnp.bfloat16).reshape(count, tokv, width)
        updated = emb[:, side].astype(jnp.float32) + jnp.einsum(
            "ptd,de->pte", context, w_out[side], preferred_element_type=jnp.float32
        )
        final = (layer_norm(updated) * gains[side, 2]).astype(jnp.bfloat16)
        head = jnp.einsum("cd,ptd->pct", w_head[side], final, preferred_element_type=jnp.float32)
        conf = 1.0 + jnp.exp(head[:, 3])
        records.append(jnp.concatenate([conf[:, None, :] * head[:, :3], conf[:, None, :]], axis=1))
    return jnp.stack(records, axis=1)


def copy_block(index_ref, source_ref, target_ref):
    target_ref[...] = source_ref[...]


def pick_sides(every, side_views):
    count = side_views.shape[0]
    part, width = every.shape[1:]
    return pl.pallas_call(
        copy_block,
        out_shape=jax.ShapeDtypeStruct((count, part, width), every.dtype),
        grid_spec=pltpu.PrefetchScalarGridSpec(
            num_scalar_prefetch=1,
            grid=(count,),
            in_specs=[pl.BlockSpec((1, part, width), lambda i, index: (index[i], 0, 0))],
            out_specs=pl.BlockSpec((1, part, width), lambda i, index: (i, 0, 0)),
        ),
    )(side_views, every)


def on_device(tokens, pairs, w_embed, w_query, w_keyval, w_out, w_head, gains):
    view_count = lax.axis_size("view")
    column_count = lax.axis_size("mp")
    me = lax.axis_index("view")
    view_dev, tokv, feat_shard = tokens.shape
    width = w_embed.shape[1]
    block_pairs = pairs.shape[0]
    pair_dev = block_pairs // column_count
    side_count = 2 * block_pairs
    cap = max(2, (side_count + view_count - 1) // view_count)
    part = tokv // column_count
    all_pairs = lax.all_gather(pairs, "view", axis=0, tiled=True)
    full = lax.all_to_all(tokens, "mp", split_axis=1, concat_axis=2, tiled=True)
    emb = jnp.dot(
        full.reshape(view_dev * part, feat_shard * column_count),
        w_embed,
        preferred_element_type=jnp.float32,
    ).astype(jnp.bfloat16).reshape(view_dev, part, width)
    every = lax.all_gather(emb, "view", axis=0, tiled=True)
    side_views = pairs.reshape(side_count)
    chosen = pick_sides(every, side_views)
    parcel = chosen.reshape(column_count, pair_dev * 2, part, width)
    arrived = lax.all_to_all(parcel, "mp", split_axis=0, concat_axis=0, tiled=False)
    sides = jnp.transpose(arrived, (1, 0, 2, 3)).reshape(pair_dev, 2, tokv, width)
    results = decode_sides(sides, w_query, w_keyval, w_out, w_head, gains)

    chunk = 4 * tokv // column_count
    shares = results.reshape(2 * pair_dev, column_count, chunk)
    shares = lax.all_to_all(shares, "mp", split_axis=1, concat_axis=0, tiled=False)
    shares = shares.reshape(side_count, chunk)
    owners = side_views // view_dev
    positions = jnp.arange(side_count, dtype=jnp.int32)
    earlier = jnp.logical_and(
        owners[:, None] == owners[None, :], positions[None, :] < positions[:, None]
    )
    slot_index = owners * cap + jnp.sum(earlier, axis=1)
    match = jnp.arange(view_count * cap, dtype=jnp.int32)[:, None] == slot_index[None, :]
    outgoing = jnp.sum(jnp.where(match[..., None], shares[None], 0.0), axis=1).reshape(view_count, cap, chunk)
    incoming = lax.all_to_all(outgoing, "view", split_axis=0, concat_axis=0, tiled=True)

    asked = all_pairs.reshape(view_count, side_count)
    mine = asked // view_dev == me
    rank = jnp.sum(
        jnp.logical_and(mine[:, None, :], positions[None, None, :] < positions[None, :, None]), axis=2
    )
    slot = jnp.arange(cap, dtype=jnp.int32)
    hit = jnp.logical_and(mine[:, None, :], rank[:, None, :] == slot[None, :, None])
    local = jnp.sum(jnp.where(hit, (asked % view_dev + 1)[:, None, :], 0), axis=2) - 1
    picks = local[None] == jnp.arange(view_dev, dtype=jnp.int32)[:, None, None]
    owned = jnp.sum(jnp.where(picks[..., None], incoming[None], 0.0), axis=(1, 2))
    gathered = lax.all_gather(owned, "mp", axis=1, tiled=True)
    return gathered.reshape(view_dev, 4, tokv)


def solution(mesh):
    return jax.shard_map(
        on_device,
        mesh=mesh,
        in_specs=(P("view", None, "mp"), P("view", None), P(), P(), P(), P(), P(), P()),
        out_specs=P("view", None, None),
        check_vma=False,
    )
```

time: 475 us -> 316 us (0.67)
  waiting for transfers between devices: 311 us -> 117 us
  Pallas kernels: 0 us -> 17.8 us
  blocking collectives: 45.8 us -> 63 us
  starting transfers between devices: 15.3 us -> 23.3 us
  local copies, waits for them, and re-layouts: 29.2 us -> 23.6 us
    all_to_all x2 -> x3, waiting for transfers between devices: 173 us -> 13.5 us  [the longest x1 8.81 us: on_device(): lax.all_to_all(outgoing, 'view', split_axis=0, concat_axis=0, tiled=True)]
    unnamed x2 -> x1, waiting for transfers between devices: 138 us -> 0.02 us
    all_gather x0 -> x1, waiting for transfers between devices: none -> 104 us  [on_device(): every = lax.all_gather(emb, 'view', axis=0, tiled=True)]
    all_gather x0 -> x2, blocking collectives: none -> 49.3 us  [the longest x1 34.5 us: on_device(): all_pairs = lax.all_gather(pairs, 'view', axis=0, tiled=True)]
    psum x1 -> x0, blocking collectives: 25.4 us -> none  [on_device(): return lax.psum(owned, 'mp')]
    pallas_call x0 -> x1, Pallas kernels: none -> 17.8 us  [pick_sides(): pl.pallas_call(copy_block, out_shape=jax.ShapeDtypeStruct((count, part, w...]
    all_to_all x2 -> x3, starting transfers between devices: 15.3 us -> 23.3 us  [the longest x1 11.2 us: on_device(): lax.all_to_all(shares, 'mp', split_axis=1, concat_axis=0, tiled=False)]
    all_to_all x1, blocking collectives: 20.4 us -> 13.7 us  [on_device(): full = lax.all_to_all(tokens, 'mp', split_axis=1, concat_axis=2, tiled=True)]
  transfers between devices with their start and end apart: 3 -> 4, of which waited for: 3 -> 3; matrix products, arithmetic and copies ran while one was open for 0% -> 1% of each run, Pallas kernels for 0% -> 0%
where the time goes in v1:
time: 316 us; the launch traced here: 315 us
  waiting for transfers between devices  117 us (37%)
  blocking collectives  63 us (20%)
  matrix products  50.7 us (16%)
  local copies, waits for them, and re-layouts  23.6 us (7%)
  starting transfers between devices  23.3 us (7%)
  Pallas kernels  17.8 us (6%)
  between operations  13.8 us (4%)
  other arithmetic  4.98 us (2%)
    all_gather x1, waiting for transfers between devices, on_device(): every = lax.all_gather(emb, 'view', axis=0, tiled=True)  104 us
    all_gather x1, blocking collectives, on_device(): all_pairs = lax.all_gather(pairs, 'view', axis=0, tiled=True)  34.5 us
    sub x2, matrix products, decode_sides(): probs = jax.nn.softmax(scores, axis=-1).astype(jnp.bfloat16)  18.7 us
    pallas_call x1, Pallas kernels, pick_sides(): pl.pallas_call(copy_block, out_shape=jax.ShapeDtypeStruct((count, part, w...  17.8 us
    all_gather x1, blocking collectives, on_device(): gathered = lax.all_gather(owned, 'mp', axis=1, tiled=True)  14.8 us
    all_to_all x1, blocking collectives, on_device(): full = lax.all_to_all(tokens, 'mp', split_axis=1, concat_axis=2, tiled=True)  13.7 us
    dot_general x2, matrix products, decode_sides(): jnp.einsum('phqk,pkhd->pqhd', probs, value_h, preferred_element_type=jnp....  12.8 us
    all_to_all x1, starting transfers between devices, on_device(): lax.all_to_all(shares, 'mp', split_axis=1, concat_axis=0, tiled=False)  11.2 us
  transfers between devices with their start and end apart: 4, of which 3 were waited for; matrix products, arithmetic and copies ran while one was open for 1% of the time, Pallas kernels for 0%

profile of v1, /device:TPU:1, one launch (start us, length us, event | category | flops | bytes accessed | tf_op | source)
XLA Modules:
  0.0 314.6 jit_solution(6523427237833108541)
XLA Ops:
  6.5 1.4 copy.111
  8.0 13.7 %all_to_all.40 = bf16[4,384,128]{2,0,1:T(4,128)(2,1)S(1)} all-to-all(bf16[4,384,128]{2,0,1:T(4,128)(2,1)S(1)} %copy.111), channel_id=1, replica_groups=mesh['view'=32,'mp'=8] {'mp'}, dimensions={1} | all-to-all | bytes 786432 | tf_op jit(solution)/shard_map/all_to_all | solution.py:88
  23.9 103.9 %all-gather.4.cloned.1.call-done.source_ref = bf16[128,48,768]{2,1,0:T(8,128)(2,1)} async-done(((bf16[4,48,768]{2,1,0:T(8,128)(2,1)}), bf16[128,48,768]{2,1,0:T(8,128)(2,1)}) %all-gather.4.cloned.1.call-update) | async-done | bytes 9437200 | tf_op jit(solution)/shard_map/all_gather | solution.py:94
  127.7 17.8 %shard_map.82 = bf16[32,48,768]{2,1,0:T(8,128)(2,1)} custom-call(s32[32]{0:T(128)} %reshape.272.index_ref, bf16[128,48,768]{2,1,0:T(8,128)(2,1)} %all-gather.4.cloned.1.call-done.source_ref), custom_call_target="tpu_custom_call" | custom-call | tf_op jit(solution)/shard_map/pallas_call | solution.py:64
  145.5 5.5 %all-to-all-start.1 = ((bf16[8,4,48,768]{3,2,1,0:T(8,128)(2,1)}), bf16[8,4,48,768]{3,2,1,0:T(8,128)(2,1)}, u32[]{:S(2)}, u32[]{:S(2)}) async-start(bf16[8,4,48,768]{3,2,1,0:T(8,128)(2,1)} %bitcast.168), calls=%async_computation.1 | async-start | bytes 4718592 | tf_op jit(solution)/shard_map/all_to_all | solution.py:98
  151.0 34.5 %all-gather = s32[32,16,2]{1,2,0:T(2,128)S(1)} all-gather(s32[1,16,2]{1,2,0:T(2,128)S(1)} %bitcast.185), channel_id=1, replica_groups=mesh['view'=32,'mp'=8] {'view'}, dimensions={0}, use_global_device_ids=true | all-gather | bytes 4224 | tf_op jit(solution)/shard_map/all_gather | solution.py:87
  188.6 1.9 copy.113
  192.4 3.7 %convolution_convert_fusion = bf16[2,384,1536]{2,1,0:T(8,128)(2,1)S(1)} fusion(bf16[2,768,1536]{2,1,0:T(8,128)(2,1)} %param.12, f32[768]{0:T(1024)S(1)} %get-tuple-element.10, f32[2,384]{1,0:T(2,128)S(1)} %add_rsqrt_fusion.2, f32[2,384]{1,0:T(2,128)S(1)} %get-tuple-element.27, bf16[2,2,384,768]{3,2,1,0:T(8,128)(2,1)S(1)} %bitcast.162), kind=kOutput, calls=%fused_computation.20 | convolution fusion | flops 1816068096 | bytes 5908480 | tf_op jit(solution)/shard_map/ptd,de->pte/dot_general | solution.py:35
  197.3 2.4 copy.121
  200.3 3.5 %convolution_convert_fusion.2 = bf16[2,384,768]{2,1,0:T(8,128)(2,1)} fusion(bf16[2,768,768]{2,1,0:T(8,128)(2,1)} %param.11, f32[768]{0:T(1024)} %get-tuple-element.14, f32[2,384]{1,0:T(2,128)S(1)} %add_rsqrt_fusion.3, f32[2,384]{1,0:T(2,128)S(1)} %copy-done.10, bf16[2,2,384,768]{3,2,1,0:T(8,128)(2,1)S(1)} %bitcast.163), kind=kOutput, calls=%fused_computation.51 | convolution fusion | flops 909508608 | bytes 3549184 | tf_op jit(solution)/shard_map/ptd,de->pte/dot_general | solution.py:32
  203.7 2.4 copy.122
  207.5 9.2 %fusion.89 = (f32[2,12,384]{2,1,0:T(8,128)}, f32[2,12,384,384]{2,3,1,0:T(8,128)}) fusion(bf16[2,384,12,64]{1,3,2,0:T(8,128)(2,1)} %bitcast.174, bf16[2,384,12,64]{1,3,2,0:T(8,128)(2,1)} %bitcast.176), kind=kOutput, calls=%fused_computation.146 | convolution fusion | flops 463602048 | bytes 16551936 | tf_op jit(solution)/shard_map/sub | solution.py:44
  216.8 6.4 %fusion.34 = bf16[2,12,64,384]{3,2,1,0:T(8,128)(2,1)S(1)} fusion(bf16[2,384,12,64]{1,3,2,0:T(8,128)(2,1)S(1)} %bitcast.172, f32[2,12,384,384]{2,3,1,0:T(8,128)} %get-tuple-element.20, f32[2,12,384]{2,1,0:T(8,128)} %get-tuple-element.19), kind=kOutput, calls=%fused_computation.49 | convolution fusion | flops 460652544 | bytes 16551936 | tf_op jit(solution)/shard_map/phqk,pkhd->pqhd/dot_general | solution.py:45
  225.8 3.8 %convolution_convert_fusion.1 = bf16[2,384,1536]{2,1,0:T(8,128)(2,1)S(1)} fusion(bf16[2,768,1536]{2,1,0:T(8,128)(2,1)} %param.12, f32[768]{0:T(1024)S(1)} %copy-done.14, f32[2,384]{1,0:T(2,128)S(1)} %copy-done.17, f32[2,384]{1,0:T(2,128)S(1)} %copy-done.11, bf16[2,2,384,768]{3,2,1,0:T(8,128)(2,1)S(1)} %bitcast.165), kind=kOutput, calls=%fused_computation.21 | convolution fusion | flops 1816068096 | bytes 5908480 | tf_op jit(solution)/shard_map/ptd,de->pte/dot_general | solution.py:35
  230.7 2.4 copy.116
  233.1 3.5 %convolution_convert_fusion.3 = bf16[2,384,768]{2,1,0:T(8,128)(2,1)} fusion(bf16[2,768,768]{2,1,0:T(8,128)(2,1)} %param.11, f32[768]{0:T(1024)} %get-tuple-element.11, f32[2,384]{1,0:T(2,128)} %copy-done.15, f32[2,384]{1,0:T(2,128)} %copy-done.8, bf16[2,2,384,768]{3,2,1,0:T(8,128)(2,1)S(1)} %bitcast.166), kind=kOutput, calls=%fused_computation.52 | convolution fusion | flops 909508608 | bytes 3549184 | tf_op jit(solution)/shard_map/ptd,de->pte/dot_general | solution.py:32
  236.6 2.4 copy.117
  240.4 9.5 %fusion.91 = (f32[2,12,384]{2,1,0:T(8,128)}, f32[2,12,384,384]{2,3,1,0:T(8,128)}) fusion(bf16[2,384,12,64]{1,3,2,0:T(8,128)(2,1)} %bitcast.175, bf16[2,384,12,64]{1,3,2,0:T(8,128)(2,1)} %bitcast.177), kind=kOutput, calls=%fused_computation.148 | convolution fusion | flops 463602048 | bytes 16551936 | tf_op jit(solution)/shard_map/sub | solution.py:44
  249.9 6.4 %fusion.35 = bf16[2,12,64,384]{3,2,1,0:T(8,128)(2,1)S(1)} fusion(bf16[2,384,12,64]{1,3,2,0:T(8,128)(2,1)S(1)} %bitcast.173, f32[2,12,384,384]{2,3,1,0:T(8,128)} %get-tuple-element.24, f32[2,12,384]{2,1,0:T(8,128)} %get-tuple-element.23), kind=kOutput, calls=%fused_computation.50 | convolution fusion | flops 460652544 | bytes 16551936 | tf_op jit(solution)/shard_map/phqk,pkhd->pqhd/dot_general | solution.py:45
  259.6 11.2 %all-to-all-start.2 = ((f32[1,4,8,192]{3,1,0,2:T(4,128)}), f32[1,4,8,192]{3,1,0,2:T(4,128)S(1)}, u32[]{:S(2)}, u32[]{:S(2)}) async-start(f32[1,4,8,192]{3,1,0,2:T(4,128)} %copy.127), calls=%async_computation.2 | async-start | bytes 65536 | tf_op jit(solution)/shard_map/all_to_all | solution.py:104
  270.8 4.7 %all-to-all-done.2 = f32[1,4,8,192]{3,1,0,2:T(4,128)S(1)} async-done(((f32[1,4,8,192]{3,1,0,2:T(4,128)}), f32[1,4,8,192]{3,1,0,2:T(4,128)S(1)}, u32[]{:S(2)}, u32[]{:S(2)}) %all-to-all-start.2) | async-done | bytes 24608 | tf_op jit(solution)/shard_map/all_to_all | solution.py:104
  276.7 6.6 %all-to-all-start.3 = ((f32[32,2,192]{2,1,0:T(2,128)}), f32[32,2,192]{2,1,0:T(2,128)S(1)}, u32[]{:S(2)}, u32[]{:S(2)}) async-start(f32[32,2,192]{2,1,0:T(2,128)} %reshape.285), calls=%async_computation.3 | async-start | bytes 131072 | tf_op jit(solution)/shard_map/all_to_all | solution.py:114
  283.3 8.8 %all-to-all-done.3 = f32[32,2,192]{2,1,0:T(2,128)S(1)} async-done(((f32[32,2,192]{2,1,0:T(2,128)}), f32[32,2,192]{2,1,0:T(2,128)S(1)}, u32[]{:S(2)}, u32[]{:S(2)}) %all-to-all-start.3) | async-done | bytes 49184 | tf_op jit(solution)/shard_map/all_to_all | solution.py:114
  292.3 14.8 %all-gather.1 = f32[8,192,4]{1,2,0:T(4,128)S(1)} all-gather(f32[1,192,4]{1,2,0:T(4,128)S(1)} %bitcast.182), channel_id=1, replica_groups=mesh['view'=32,'mp'=8] {'mp'}, dimensions={0}, use_global_device_ids=true | all-gather | bytes 27648 | tf_op jit(solution)/shard_map/all_gather | solution.py:126
  (103 shorter events, 20.6 us)
Async XLA Ops:
  6.5 15.4 %copy-start = (bf16[1024,768]{1,0:T(8,128)(2,1)S(1)}, bf16[1024,768]{1,0:T(8,128)(2,1)}, u32[]{:S(2)}) copy-start(bf16[1024,768]{1,0:T(8,128)(2,1)} %param.10) | copy-start | bytes 4718596
  6.5 16.6 %copy-start.12 = (s32[16,2]{0,1:T(2,128)S(1)}, s32[16,2]{0,1:T(2,128)}, u32[]{:S(2)}) copy-start(s32[16,2]{0,1:T(2,128)} %param.9) | copy-start | bytes 388
  6.5 121.2 %all-gather.4.cloned.1.call-start = ((), (), s32[]{:S(2)}) async-start(), calls=%async_computation.4 | async-start | bytes 9732096 | tf_op jit(solution)/shard_map/all_gather | solution.py:94
  145.5 40.3 %copy-start.18 = (s32[32]{0:T(128)S(1)}, s32[32]{0:T(128)}, u32[]{:S(2)}) copy-start(s32[32]{0:T(128)} %reshape.272.index_ref) | copy-start | bytes 388
  145.5 41.9 %copy-start.5 = (f32[2,3,768]{2,0,1:T(2,128)S(1)}, f32[2,3,768]{2,0,1:T(2,128)}, u32[]{:S(2)}) copy-start(f32[2,3,768]{2,0,1:T(2,128)} %param.15) | copy-start | bytes 55300
  145.5 43.1 %all-to-all-start.1 = ((bf16[8,4,48,768]{3,2,1,0:T(8,128)(2,1)}), bf16[8,4,48,768]{3,2,1,0:T(8,128)(2,1)}, u32[]{:S(2)}, u32[]{:S(2)}) async-start(bf16[8,4,48,768]{3,2,1,0:T(8,128)(2,1)} %bitcast.168), calls=%async_computation.1 | async-start | bytes 4718592 | tf_op jit(solution)/shard_map/all_to_all | solution.py:98
  190.9 0.9 copy-start.8
  190.9 0.9 copy-start.9
  197.3 3.0 copy-start.10
  199.7 0.6 copy-start.16
  207.5 9.2 %copy-start.2 = (bf16[2,384,768]{1,2,0:T(8,128)(2,1)S(1)}, bf16[2,384,768]{1,2,0:T(8,128)(2,1)}, u32[]{:S(2)}) copy-start(bf16[2,384,768]{1,2,0:T(8,128)(2,1)} %copy.121) | copy-start | bytes 3538948
  216.8 6.4 %copy-start.19 = (bf16[2,768,768]{2,1,0:T(8,128)(2,1)S(1)}, bf16[2,768,768]{2,1,0:T(8,128)(2,1)}, u32[]{:S(2)}) copy-start(bf16[2,768,768]{2,1,0:T(8,128)(2,1)} %param.13) | copy-start | bytes 7077892
  224.4 0.7 copy-start.6
  224.5 1.3 copy-start.11
  224.5 1.3 copy-start.14
  224.5 1.3 copy-start.17
  240.4 9.5 %copy-start.3 = (bf16[2,384,768]{1,2,0:T(8,128)(2,1)S(1)}, bf16[2,384,768]{1,2,0:T(8,128)(2,1)}, u32[]{:S(2)}) copy-start(bf16[2,384,768]{1,2,0:T(8,128)(2,1)} %copy.116) | copy-start | bytes 3538948
  249.9 6.4 %copy-start.20 = (bf16[2,768,768]{2,1,0:T(8,128)(2,1)S(1)}, bf16[2,768,768]{2,1,0:T(8,128)(2,1)}, u32[]{:S(2)}) copy-start(bf16[2,768,768]{2,1,0:T(8,128)(2,1)} %param.13) | copy-start | bytes 7077892
  257.5 0.7 copy-start.7
  257.6 13.3 %copy-start.13 = (s32[32,2]{0,1:T(2,128)S(1)}, s32[32,2]{0,1:T(2,128)}, u32[]{:S(2)}) copy-start(s32[32,2]{0,1:T(2,128)} %select_reduce_fusion.2) | copy-start | bytes 772
  257.6 18.0 %copy-start.4 = (pred[64,32]{1,0:T(8,128)(4,1)S(1)}, pred[64,32]{1,0:T(8,128)(4,1)}, u32[]{:S(2)}) copy-start(pred[64,32]{1,0:T(8,128)(4,1)} %iota_compare_fusion) | copy-start | bytes 6148
  257.6 50.2 %copy-start.1 = (bf16[1024,768]{1,0:T(8,128)(2,1)S(1)}, bf16[1024,768]{1,0:T(8,128)(2,1)}, u32[]{:S(2)}) copy-start(bf16[1024,768]{1,0:T(8,128)(2,1)} %param.10) | copy-start | bytes 4718596
  259.6 15.9 %all-to-all-start.2 = ((f32[1,4,8,192]{3,1,0,2:T(4,128)}), f32[1,4,8,192]{3,1,0,2:T(4,128)S(1)}, u32[]{:S(2)}, u32[]{:S(2)}) async-start(f32[1,4,8,192]{3,1,0,2:T(4,128)} %copy.127), calls=%async_computation.2 | async-start | bytes 65536 | tf_op jit(solution)/shard_map/all_to_all | solution.py:104
  276.7 15.4 %all-to-all-start.3 = ((f32[32,2,192]{2,1,0:T(2,128)}), f32[32,2,192]{2,1,0:T(2,128)S(1)}, u32[]{:S(2)}, u32[]{:S(2)}) async-start(f32[32,2,192]{2,1,0:T(2,128)} %reshape.285), calls=%async_computation.3 | async-start | bytes 131072 | tf_op jit(solution)/shard_map/all_to_all | solution.py:114
  (1 other events, 0.6 us)
Sparse Core Ops, SparseCore 0:
  23.3 104.3 all-gather.3

commit v2 on v1

--- a/solution.py
+++ b/solution.py
@@ -1,3 +1,5 @@
+import functools
+
 import jax
 import jax.numpy as jnp
 from jax import lax
@@ -54,49 +56,302 @@
     return jnp.stack(records, axis=1)
 
 
-def copy_block(index_ref, source_ref, target_ref):
-    target_ref[...] = source_ref[...]
-
-
-def pick_sides(every, side_views):
+NY = 4
+ROWS = 16
+MESH = pl.DeviceIdType.MESH
+
+
+def remote(source, target, send, arrive, device):
+    return pltpu.make_async_remote_copy(
+        src_ref=source,
+        dst_ref=target,
+        send_sem=send,
+        recv_sem=arrive,
+        device_id=device,
+        device_id_type=MESH,
+    )
+
+
+def gather_kernel(nz, nm, chunks, tokens, wanted, places, w_embed, out, full, w_near, w_held, slots, parcels, *rest):
+    pools = rest[:chunks]
+    rest = rest[chunks:]
+    held = [rest[c * nz : (c + 1) * nz] for c in range(chunks)]
+    rest = rest[chunks * nz :]
+    (t_send, t_recv, w_send, w_recv, z_send, z_recv, y_send, y_recv, f_send, f_recv, x_send, x_recv, local) = rest
+    view = lax.axis_index("view")
+    me = lax.axis_index("mp")
+    z = view // NY
+    y = view % NY
+    part = tokens.shape[1] // nm
+    feat = tokens.shape[2]
+    view_dev = tokens.shape[0]
+    sides = places.shape[0] // nm
+
+    def at_z(step):
+        return (lax.rem(z + step + nz, nz) * NY + y, me)
+
+    def at_y(step):
+        return (z * NY + lax.rem(y + step + NY, NY), me)
+
+    def at_m(step):
+        return (view, lax.rem(me + step, nm))
+
+    barrier = pltpu.get_barrier_semaphore()
+    peers = [at_m(o) for o in range(1, nm)] + [at_z(1), at_z(-1)] + [at_y(o) for o in range(1, NY)]
+    for peer in peers:
+        pl.semaphore_signal(barrier, inc=1, device_id=peer, device_id_type=MESH)
+    pl.semaphore_wait(barrier, len(peers))
+
+    sent = []
+
+    def start(copy):
+        copy.start()
+        sent.append(copy)
+        return copy
+
+    arriving = []
+    for o in range(1, nm):
+        j = lax.rem(me + o, nm)
+        arriving.append(
+            start(
+                remote(
+                    tokens.at[:, pl.ds(pl.multiple_of(j * part, ROWS), part), :],
+                    full.at[:, :, pl.ds(pl.multiple_of(me * feat, 128), feat)],
+                    t_send.at[o],
+                    t_recv.at[o],
+                    at_m(o),
+                )
+            )
+        )
+    own = pltpu.make_async_copy(
+        tokens.at[:, pl.ds(pl.multiple_of(me * part, ROWS), part), :],
+        full.at[:, :, pl.ds(pl.multiple_of(me * feat, 128), feat)],
+        local.at[0],
+    )
+    own.start()
+    asking = [
+        start(remote(wanted, w_near.at[NY - o], w_send.at[o], w_recv.at[NY - o], at_y(o)))
+        for o in range(1, NY)
+    ]
+    own_wanted = pltpu.make_async_copy(wanted, w_near.at[0], local.at[1])
+    own_wanted.start()
+    own_wanted.wait()
+    for copy in asking:
+        copy.wait_recv()
+    to_scalars = pltpu.make_async_copy(w_near, w_held, local.at[2])
+    to_scalars.start()
+    to_scalars.wait()
+    own.wait()
+    for copy in arriving:
+        copy.wait_recv()
+    for c in range(chunks):
+        rows = full[:, c * ROWS : (c + 1) * ROWS, :].reshape(view_dev * ROWS, nm * feat)
+        emb = jnp.dot(rows, w_embed[...], preferred_element_type=jnp.float32)
+        held[c][0][...] = emb.astype(jnp.bfloat16).reshape(view_dev, ROWS, -1)
+
+    up = [nz // 2 if c % 2 == 0 else (nz - 1) // 2 for c in range(chunks)]
+    down = [nz - 1 - u for u in up]
+    steps = max(nz // 2, 1) + 1
+    lag = 2
+    z_copy, y_copy, f_copy, x_copy = {}, {}, {}, {}
+
+    def z_forward(c, d, way):
+        target = (d - way) % nz
+        z_copy[c, target] = start(
+            remote(
+                held[c][d],
+                held[c][target],
+                z_send.at[c, target],
+                z_recv.at[c, target],
+                at_z(way),
+            )
+        )
+
+    def chosen(c, d, dy, r):
+        owner = lax.rem(z + d, nz) * NY + y
+        return held[c][d][w_held[dy, 0, owner * 2 + r]]
+
+    def y_start(c, d):
+        slots[c, 0, d, 0] = chosen(c, d, 1, 0)
+        slots[c, 0, d, 1] = chosen(c, d, 1, 1)
+        slots[c, 0, d, 2] = chosen(c, d, 2, 0)
+        y_copy[c, 0, d] = start(
+            remote(
+                slots.at[c, 0, d],
+                pools[c].at[pl.ds(3 * d, 3)],
+                y_send.at[c, 0, d],
+                y_recv.at[c, 0, d],
+                at_y(1),
+            )
+        )
+        slots[c, 1, d, 0] = chosen(c, d, 3, 0)
+        slots[c, 1, d, 1] = chosen(c, d, 3, 1)
+        slots[c, 1, d, 2] = chosen(c, d, 2, 1)
+        y_copy[c, 1, d] = start(
+            remote(
+                slots.at[c, 1, d],
+                pools[c].at[pl.ds(3 * nz + 3 * d, 3)],
+                y_send.at[c, 1, d],
+                y_recv.at[c, 1, d],
+                at_y(-1),
+            )
+        )
+        pools[c][8 * nz + 2 * d] = chosen(c, d, 0, 0)
+        pools[c][8 * nz + 2 * d + 1] = chosen(c, d, 0, 1)
+
+    def y_forward(c, d):
+        for way in range(2):
+            y_copy[c, way, d].wait_recv()
+            f_copy[c, way, d] = start(
+                remote(
+                    pools[c].at[pl.ds(3 * nz * way + 3 * d + 2, 1)],
+                    pools[c].at[pl.ds(6 * nz + nz * way + d, 1)],
+                    f_send.at[c, way, d],
+                    f_recv.at[c, way, d],
+                    at_y(1 - 2 * way),
+                )
+            )
+
+    def offsets(c, t):
+        found = [0] if t == 0 else []
+        if 1 <= t <= up[c]:
+            found.append(nz - t)
+        if 1 <= t <= down[c]:
+            found.append(t)
+        return found
+
+    def x_start(c):
+        for d in range(nz):
+            for way in range(2):
+                f_copy[c, way, d].wait_recv()
+        for k in range(nm * sides):
+            parcels[c, k] = pools[c][places[k]]
+        for o in range(1, nm):
+            j = lax.rem(me + o, nm)
+            x_copy[c, o] = start(
+                remote(
+                    parcels.at[c, pl.ds(j * sides, sides)],
+                    out.at[:, pl.ds(pl.multiple_of(me * part + c * ROWS, ROWS), ROWS), :],
+                    x_send.at[c, o],
+                    x_recv.at[c, o],
+                    at_m(o),
+                )
+            )
+        x_copy[c, 0] = pltpu.make_async_copy(
+            parcels.at[c, pl.ds(me * sides, sides)],
+            out.at[:, pl.ds(pl.multiple_of(me * part + c * ROWS, ROWS), ROWS), :],
+            local.at[3 + c],
+        )
+        x_copy[c, 0].start()
+
+    order = [(c, t) for c in range(chunks) for t in range(steps)]
+    for i in range(len(order) + 2 * lag):
+        if i < len(order):
+            c, t = order[i]
+            for d in offsets(c, t):
+                if d:
+                    z_copy[c, d].wait_recv()
+                if t < up[c] and (t == 0 or d == nz - t):
+                    z_forward(c, d, 1)
+                if t < down[c] and (t == 0 or d == t):
+                    z_forward(c, d, -1)
+            for d in offsets(c, t):
+                y_start(c, d)
+        if 0 <= i - lag < len(order):
+            c, t = order[i - lag]
+            for d in offsets(c, t):
+                y_forward(c, d)
+        if 0 <= i - 2 * lag < len(order):
+            c, t = order[i - 2 * lag]
+            if t == steps - 1:
+                x_start(c)
+    for c in range(chunks):
+        x_copy[c, 0].wait()
+        for o in range(1, nm):
+            x_copy[c, o].wait_recv()
+    for copy in sent:
+        copy.wait_send()
+
+
+def gather_sides(tokens, wanted, places, w_embed):
+    nz = lax.axis_size("view") // NY
+    nm = lax.axis_size("mp")
+    view_dev, tokv, feat = tokens.shape
+    width = w_embed.shape[1]
+    part = tokv // nm
+    chunks = part // ROWS
+    count = places.shape[0]
+    block = (ROWS, width)
+    vmem = pl.BlockSpec(memory_space=pltpu.VMEM)
+    dma = pltpu.SemaphoreType.DMA
+    return pl.pallas_call(
+        functools.partial(gather_kernel, nz, nm, chunks),
+        out_shape=jax.ShapeDtypeStruct((count // nm, tokv, width), jnp.bfloat16),
+        in_specs=[vmem, vmem, pl.BlockSpec(memory_space=pltpu.SMEM), vmem],
+        out_specs=vmem,
+        scratch_shapes=[
+            pltpu.VMEM((view_dev, part, nm * feat), jnp.bfloat16),
+            pltpu.VMEM((NY,) + wanted.shape, jnp.int32),
+            pltpu.SMEM((NY,) + wanted.shape, jnp.int32),
+            pltpu.VMEM((chunks, 2, nz, 3) + block, jnp.bfloat16),
+            pltpu.VMEM((chunks, count) + block, jnp.bfloat16),
+        ]
+        + [pltpu.VMEM((10 * nz,) + block, jnp.bfloat16)] * chunks
+        + [pltpu.VMEM((view_dev,) + block, jnp.bfloat16)] * (chunks * nz)
+        + [dma((nm,))] * 2
+        + [dma((NY,))] * 2
+        + [dma((chunks, nz))] * 2
+        + [dma((chunks, 2, nz))] * 4
+        + [dma((chunks, nm))] * 2
+        + [dma((3 + chunks,))],
+        compiler_params=pltpu.CompilerParams(
+            collective_id=0, has_side_effects=True, vmem_limit_bytes=48 * 2**20
+        ),
+    )(tokens, wanted, places, w_embed)
+
+
+def plan_sides(side_views, view_dev, cap):
+    view_count = lax.axis_size("view")
+    nz = view_count // NY
+    me = lax.axis_index("view")
     count = side_views.shape[0]
-    part, width = every.shape[1:]
-    return pl.pallas_call(
-        copy_block,
-        out_shape=jax.ShapeDtypeStruct((count, part, width), every.dtype),
-        grid_spec=pltpu.PrefetchScalarGridSpec(
-            num_scalar_prefetch=1,
-            grid=(count,),
-            in_specs=[pl.BlockSpec((1, part, width), lambda i, index: (index[i], 0, 0))],
-            out_specs=pl.BlockSpec((1, part, width), lambda i, index: (i, 0, 0)),
+    owners = side_views // view_dev
+    positions = jnp.arange(count, dtype=jnp.int32)
+    earlier = jnp.logical_and(
+        owners[:, None] == owners[None, :], positions[None, :] < positions[:, None]
+    )
+    rank = jnp.sum(earlier, axis=1)
+    slot_index = owners * cap + rank
+    match = jnp.arange(128, dtype=jnp.int32)[:, None] == slot_index[None, :]
+    wanted = jnp.sum(jnp.where(match, (side_views % view_dev)[None, :], 0), axis=1)
+    wanted = jnp.broadcast_to(wanted[None, :], (8, 128))
+    d = (owners // NY - me // NY + nz) % nz
+    rel = (owners % NY - me % NY + NY) % NY
+    places = jnp.where(
+        rel == 0,
+        8 * nz + 2 * d + rank,
+        jnp.where(
+            rel == 3,
+            3 * d + rank,
+            jnp.where(rel == 1, 3 * nz + 3 * d + rank, 6 * nz + nz * rank + d),
         ),
-    )(side_views, every)
+    )
+    return wanted, places
 
 
 def on_device(tokens, pairs, w_embed, w_query, w_keyval, w_out, w_head, gains):
     view_count = lax.axis_size("view")
     column_count = lax.axis_size("mp")
     me = lax.axis_index("view")
-    view_dev, tokv, feat_shard = tokens.shape
-    width = w_embed.shape[1]
+    view_dev, tokv, unused = tokens.shape
     block_pairs = pairs.shape[0]
     pair_dev = block_pairs // column_count
     side_count = 2 * block_pairs
     cap = max(2, (side_count + view_count - 1) // view_count)
-    part = tokv // column_count
     all_pairs = lax.all_gather(pairs, "view", axis=0, tiled=True)
-    full = lax.all_to_all(tokens, "mp", split_axis=1, concat_axis=2, tiled=True)
-    emb = jnp.dot(
-        full.reshape(view_dev * part, feat_shard * column_count),
-        w_embed,
-        preferred_element_type=jnp.float32,
-    ).astype(jnp.bfloat16).reshape(view_dev, part, width)
-    every = lax.all_gather(emb, "view", axis=0, tiled=True)
     side_views = pairs.reshape(side_count)
-    chosen = pick_sides(every, side_views)
-    parcel = chosen.reshape(column_count, pair_dev * 2, part, width)
-    arrived = lax.all_to_all(parcel, "mp", split_axis=0, concat_axis=0, tiled=False)
-    sides = jnp.transpose(arrived, (1, 0, 2, 3)).reshape(pair_dev, 2, tokv, width)
+    wanted, places = plan_sides(side_views, view_dev, cap)
+    sides = gather_sides(tokens, wanted, places, w_embed).reshape(pair_dev, 2, tokv, -1)
     results = decode_sides(sides, w_query, w_keyval, w_out, w_head, gains)
 
     chunk = 4 * tokv // column_count

time: 316 us -> 237 us (0.75)
  waiting for transfers between devices: 117 us -> 8.81 us
  Pallas kernels: 17.8 us -> 86.2 us
  starting transfers between devices: 23.3 us -> 7.54 us
  between operations: 13.8 us -> 0.48 us
  blocking collectives: 63 us -> 57.3 us
    all_gather x1 -> x0, waiting for transfers between devices: 104 us -> none  [on_device(): every = lax.all_gather(emb, 'view', axis=0, tiled=True)]
    pallas_call x1, Pallas kernels: 17.8 us -> 86.2 us  [gather_sides(): pl.pallas_call(functools.partial(gather_kernel, nz, nm, chunks), out_shap...]
    all_to_all x1 -> x0, blocking collectives: 13.7 us -> none  [on_device(): full = lax.all_to_all(tokens, 'mp', split_axis=1, concat_axis=2, tiled=True)]
    all_gather x1, blocking collectives: 14.8 us -> 24.5 us  [on_device(): gathered = lax.all_gather(owned, 'mp', axis=1, tiled=True)]
    all_to_all x1, starting transfers between devices: 11.2 us -> 3.28 us  [on_device(): lax.all_to_all(shares, 'mp', split_axis=1, concat_axis=0, tiled=False)]
    all_to_all x1 -> x0, starting transfers between devices: 5.47 us -> none  [on_device(): lax.all_to_all(parcel, 'mp', split_axis=0, concat_axis=0, tiled=False)]
    all_to_all x1, waiting for transfers between devices: 4.71 us -> 0.01 us  [on_device(): lax.all_to_all(shares, 'mp', split_axis=1, concat_axis=0, tiled=False)]
  transfers between devices with their start and end apart: 4 -> 2, of which waited for: 3 -> 1; matrix products, arithmetic and copies ran while one was open for 1% -> 0% of each run, Pallas kernels for 0% -> 0%
where the time goes in v2:
time: 237 us; the launch traced here: 236 us
  Pallas kernels  86.2 us (36%)
  blocking collectives  57.3 us (24%)
  matrix products  47.7 us (20%)
  local copies, waits for them, and re-layouts  23.9 us (10%)
  waiting for transfers between devices  8.81 us (4%)
  starting transfers between devices  7.54 us (3%)
  other arithmetic  3.91 us (2%)
    pallas_call x1, Pallas kernels, gather_sides(): pl.pallas_call(functools.partial(gather_kernel, nz, nm, chunks), out_shap...  86.2 us
    all_gather x1, blocking collectives, on_device(): all_pairs = lax.all_gather(pairs, 'view', axis=0, tiled=True)  32.9 us
    all_gather x1, blocking collectives, on_device(): gathered = lax.all_gather(owned, 'mp', axis=1, tiled=True)  24.5 us
    sub x2, matrix products, decode_sides(): probs = jax.nn.softmax(scores, axis=-1).astype(jnp.bfloat16)  18.5 us
    dot_general x2, matrix products, decode_sides(): jnp.einsum('phqk,pkhd->pqhd', probs, value_h, preferred_element_type=jnp....  12.8 us
    all_to_all x1, waiting for transfers between devices, on_device(): lax.all_to_all(outgoing, 'view', split_axis=0, concat_axis=0, tiled=True)  8.81 us
    dot_general x2, matrix products, decode_sides(): jnp.einsum('ptd,de->pte', query_in, w_query[side], preferred_element_type...  6.95 us
    dot_general x2, matrix products, decode_sides(): jnp.einsum('ptd,de->pte', memory_in, w_keyval[side], preferred_element_ty...  5.9 us
  transfers between devices with their start and end apart: 2, of which 1 were waited for; matrix products, arithmetic and copies ran while one was open for 0% of the time, Pallas kernels for 0%

profile of v2, /device:TPU:1, one launch (start us, length us, event | category | flops | bytes accessed | tf_op | source)
XLA Modules:
  0.0 235.9 jit_solution(16383086261786317521)
XLA Ops:
  0.0 1.4 slice_reduce_fusion.3
  2.6 1.4 copy-done
  5.0 86.2 %shard_map.82 = bf16[4,384,768]{2,1,0:T(8,128)(2,1)S(1)} custom-call(bf16[4,384,128]{2,1,0:T(8,128)(2,1)S(1)} %copy-done.1, s32[8,128]{1,0:T(8,128)S(1)} %broadcast_in_dim.63.wanted, s32[32]{0:T(128)S(1)} %get-tuple-element.19.places, bf16[1024,768]{1,0:T(8,128)(2,1)S(1)} %copy-done), custom_call_target="tpu_custom_call" | custom-call | tf_op jit(solution)/shard_map/pallas_call | solution.py:287
  93.6 2.1 convolution_convert_fusion
  96.9 2.4 %copy.110 = bf16[2,384,768]{1,2,0:T(8,128)(2,1)} copy(bf16[2,384,768]{2,1,0:T(8,128)(2,1)} %get-tuple-element.18) | data formatting | bytes 2359296 | tf_op jit(solution)/shard_map/slice | solution.py:42
  99.9 3.5 %convolution_convert_fusion.2 = bf16[2,384,768]{2,1,0:T(8,128)(2,1)} fusion(bf16[2,768,768]{2,1,0:T(8,128)(2,1)} %param.11, f32[768]{0:T(1024)} %get-tuple-element.14, f32[2,384]{1,0:T(2,128)S(1)} %add_rsqrt_fusion.3, f32[2,384]{1,0:T(2,128)S(1)} %copy-done.8, bf16[2,2,384,768]{3,2,1,0:T(8,128)(2,1)S(1)} %bitcast.151), kind=kOutput, calls=%fused_computation.51 | convolution fusion | flops 909508608 | bytes 3549184 | tf_op jit(solution)/shard_map/ptd,de->pte/dot_general | solution.py:34
  103.4 2.4 %copy.111 = bf16[2,384,768]{1,2,0:T(8,128)(2,1)} copy(bf16[2,384,768]{2,1,0:T(8,128)(2,1)} %convolution_convert_fusion.2) | data formatting | bytes 2359296 | tf_op jit(solution)/shard_map/convert_element_type | solution.py:36
  105.8 1.4 copy.112
  107.2 9.2 %fusion.91 = (f32[2,12,384]{2,1,0:T(8,128)}, f32[2,12,384,384]{2,3,1,0:T(8,128)}) fusion(bf16[2,384,12,64]{1,3,2,0:T(8,128)(2,1)} %bitcast.158, bf16[2,384,12,64]{1,3,2,0:T(8,128)(2,1)} %bitcast.160), kind=kOutput, calls=%fused_computation.164 | convolution fusion | flops 463602048 | bytes 16551936 | tf_op jit(solution)/shard_map/sub | solution.py:46
  116.4 6.4 %fusion.34 = bf16[2,12,64,384]{3,2,1,0:T(8,128)(2,1)S(1)} fusion(bf16[2,384,12,64]{1,3,2,0:T(8,128)(2,1)S(1)} %bitcast.156, f32[2,12,384,384]{2,3,1,0:T(8,128)} %get-tuple-element.24, f32[2,12,384]{2,1,0:T(8,128)} %get-tuple-element.23), kind=kOutput, calls=%fused_computation.49 | convolution fusion | flops 460652544 | bytes 16551936 | tf_op jit(solution)/shard_map/phqk,pkhd->pqhd/dot_general | solution.py:47
  122.8 1.2 fusion.92
  125.4 3.8 %convolution_convert_fusion.1 = bf16[2,384,1536]{2,1,0:T(8,128)(2,1)S(1)} fusion(bf16[2,768,1536]{2,1,0:T(8,128)(2,1)} %param.12, f32[768]{0:T(1024)S(1)} %copy-done.11, f32[2,384]{1,0:T(2,128)S(1)} %copy-done.14, f32[2,384]{1,0:T(2,128)S(1)} %copy-done.9, bf16[2,2,384,768]{3,2,1,0:T(8,128)(2,1)S(1)} %bitcast.153), kind=kOutput, calls=%fused_computation.21 | convolution fusion | flops 1816068096 | bytes 5908480 | tf_op jit(solution)/shard_map/ptd,de->pte/dot_general | solution.py:37
  130.4 2.4 %copy.105 = bf16[2,384,768]{1,2,0:T(8,128)(2,1)} copy(bf16[2,384,768]{2,1,0:T(8,128)(2,1)} %get-tuple-element.16) | data formatting | bytes 2359296 | tf_op jit(solution)/shard_map/slice | solution.py:42
  132.8 3.5 %convolution_convert_fusion.3 = bf16[2,384,768]{2,1,0:T(8,128)(2,1)} fusion(bf16[2,768,768]{2,1,0:T(8,128)(2,1)} %param.11, f32[768]{0:T(1024)} %get-tuple-element.11, f32[2,384]{1,0:T(2,128)} %copy-done.12, f32[2,384]{1,0:T(2,128)} %copy-done.6, bf16[2,2,384,768]{3,2,1,0:T(8,128)(2,1)S(1)} %bitcast.154), kind=kOutput, calls=%fused_computation.52 | convolution fusion | flops 909508608 | bytes 3549184 | tf_op jit(solution)/shard_map/ptd,de->pte/dot_general | solution.py:34
  136.2 2.4 %copy.106 = bf16[2,384,768]{1,2,0:T(8,128)(2,1)} copy(bf16[2,384,768]{2,1,0:T(8,128)(2,1)} %convolution_convert_fusion.3) | data formatting | bytes 2359296 | tf_op jit(solution)/shard_map/convert_element_type | solution.py:36
  138.6 1.4 copy.107
  140.1 9.2 %fusion.93 = (f32[2,12,384]{2,1,0:T(8,128)}, f32[2,12,384,384]{2,3,1,0:T(8,128)}) fusion(bf16[2,384,12,64]{1,3,2,0:T(8,128)(2,1)} %bitcast.159, bf16[2,384,12,64]{1,3,2,0:T(8,128)(2,1)} %bitcast.161), kind=kOutput, calls=%fused_computation.166 | convolution fusion | flops 463602048 | bytes 16551936 | tf_op jit(solution)/shard_map/sub | solution.py:46
  149.3 6.4 %fusion.35 = bf16[2,12,64,384]{3,2,1,0:T(8,128)(2,1)S(1)} fusion(bf16[2,384,12,64]{1,3,2,0:T(8,128)(2,1)S(1)} %bitcast.157, f32[2,12,384,384]{2,3,1,0:T(8,128)} %get-tuple-element.28, f32[2,12,384]{2,1,0:T(8,128)} %get-tuple-element.27), kind=kOutput, calls=%fused_computation.50 | convolution fusion | flops 460652544 | bytes 16551936 | tf_op jit(solution)/shard_map/phqk,pkhd->pqhd/dot_general | solution.py:47
  155.7 1.2 fusion.94
  159.0 3.3 %all-to-all-start = ((f32[1,4,8,192]{3,1,0,2:T(4,128)}), f32[1,4,8,192]{3,1,0,2:T(4,128)S(1)}, u32[]{:S(2)}, u32[]{:S(2)}) async-start(f32[1,4,8,192]{3,1,0,2:T(4,128)} %copy.116), calls=%async_computation | async-start | bytes 65536 | tf_op jit(solution)/shard_map/all_to_all | solution.py:359
  162.4 32.9 %all-gather = s32[32,16,2]{1,2,0:T(2,128)S(1)} all-gather(s32[1,16,2]{1,2,0:T(2,128)S(1)} %bitcast.169), channel_id=1, replica_groups=mesh['view'=32,'mp'=8] {'view'}, dimensions={0}, use_global_device_ids=true | all-gather | bytes 4224 | tf_op jit(solution)/shard_map/all_gather | solution.py:351
  197.5 4.3 %all-to-all-start.1 = ((f32[32,2,192]{2,1,0:T(2,128)}), f32[32,2,192]{2,1,0:T(2,128)S(1)}, u32[]{:S(2)}, u32[]{:S(2)}) async-start(f32[32,2,192]{2,1,0:T(2,128)} %reshape.294), calls=%async_computation.1 | async-start | bytes 131072 | tf_op jit(solution)/shard_map/all_to_all | solution.py:369
  201.8 8.8 %all-to-all-done.1 = f32[32,2,192]{2,1,0:T(2,128)S(1)} async-done(((f32[32,2,192]{2,1,0:T(2,128)}), f32[32,2,192]{2,1,0:T(2,128)S(1)}, u32[]{:S(2)}, u32[]{:S(2)}) %all-to-all-start.1) | async-done | bytes 49184 | tf_op jit(solution)/shard_map/all_to_all | solution.py:369
  210.7 24.5 %all-gather.1 = f32[8,192,4]{1,2,0:T(4,128)S(1)} all-gather(f32[1,192,4]{1,2,0:T(4,128)S(1)} %bitcast.166), channel_id=1, replica_groups=mesh['view'=32,'mp'=8] {'mp'}, dimensions={0}, use_global_device_ids=true | all-gather | bytes 27648 | tf_op jit(solution)/shard_map/all_gather | solution.py:381
  (93 shorter events, 13.7 us)
Async XLA Ops:
  2.5 88.7 %copy-start.15 = (s32[32]{0:T(128)}, s32[32]{0:T(128)S(1)}, u32[]{:S(2)}) copy-start(s32[32]{0:T(128)S(1)} %get-tuple-element.20) | copy-start | bytes 388
  2.6 1.4 copy-start
  4.0 1.0 copy-start.1
  91.3 2.3 copy-start.17
  91.7 0.9 copy-start.6
  91.7 0.9 copy-start.7
  92.5 0.6 copy-start.12
  96.9 3.0 %copy-start.8 = (f32[2,384]{1,0:T(2,128)S(1)}, f32[2,384]{1,0:T(2,128)}, u32[]{:S(2)}) copy-start(f32[2,384]{1,0:T(2,128)} %copy-done.7) | copy-start | bytes 9220
  99.3 0.6 copy-start.13
  107.2 9.2 %copy-start.2 = (bf16[2,384,768]{1,2,0:T(8,128)(2,1)S(1)}, bf16[2,384,768]{1,2,0:T(8,128)(2,1)}, u32[]{:S(2)}) copy-start(bf16[2,384,768]{1,2,0:T(8,128)(2,1)} %copy.110) | copy-start | bytes 3538948
  116.4 6.4 %copy-start.18 = (bf16[2,768,768]{2,1,0:T(8,128)(2,1)S(1)}, bf16[2,768,768]{2,1,0:T(8,128)(2,1)}, u32[]{:S(2)}) copy-start(bf16[2,768,768]{2,1,0:T(8,128)(2,1)} %param.13) | copy-start | bytes 7077892
  124.1 0.7 copy-start.4
  124.1 1.3 copy-start.9
  124.1 1.3 copy-start.11
  124.1 1.3 copy-start.14
  140.0 9.2 %copy-start.3 = (bf16[2,384,768]{1,2,0:T(8,128)(2,1)S(1)}, bf16[2,384,768]{1,2,0:T(8,128)(2,1)}, u32[]{:S(2)}) copy-start(bf16[2,384,768]{1,2,0:T(8,128)(2,1)} %copy.105) | copy-start | bytes 3538948
  149.3 6.4 %copy-start.19 = (bf16[2,768,768]{2,1,0:T(8,128)(2,1)S(1)}, bf16[2,768,768]{2,1,0:T(8,128)(2,1)}, u32[]{:S(2)}) copy-start(bf16[2,768,768]{2,1,0:T(8,128)(2,1)} %param.13) | copy-start | bytes 7077892
  157.0 0.7 copy-start.5
  157.0 5.3 %copy-start.16 = (s32[32]{0:T(128)S(1)}, s32[32]{0:T(128)}, u32[]{:S(2)}) copy-start(s32[32]{0:T(128)} %copy-done.15) | copy-start | bytes 388
  157.0 5.4 %copy-start.10 = (s32[16,2]{0,1:T(2,128)S(1)}, s32[16,2]{0,1:T(2,128)}, u32[]{:S(2)}) copy-start(s32[16,2]{0,1:T(2,128)} %param.9) | copy-start | bytes 388
  159.0 37.3 %all-to-all-start = ((f32[1,4,8,192]{3,1,0,2:T(4,128)}), f32[1,4,8,192]{3,1,0,2:T(4,128)S(1)}, u32[]{:S(2)}, u32[]{:S(2)}) async-start(f32[1,4,8,192]{3,1,0,2:T(4,128)} %copy.116), calls=%async_computation | async-start | bytes 65536 | tf_op jit(solution)/shard_map/all_to_all | solution.py:359
  197.5 13.1 %all-to-all-start.1 = ((f32[32,2,192]{2,1,0:T(2,128)}), f32[32,2,192]{2,1,0:T(2,128)S(1)}, u32[]{:S(2)}, u32[]{:S(2)}) async-start(f32[32,2,192]{2,1,0:T(2,128)} %reshape.294), calls=%async_computation.1 | async-start | bytes 131072 | tf_op jit(solution)/shard_map/all_to_all | solution.py:369

commit v3 on v2

--- a/solution.py
+++ b/solution.py
@@ -8,52 +8,6 @@
 from jax.sharding import PartitionSpec as P
 
 HEADS = 12
-
-
-def layer_norm(values):
-    mean = jnp.mean(values, axis=-1, keepdims=True)
-    centred = values - mean
-    var = jnp.mean(centred * centred, axis=-1, keepdims=True)
-    return centred * lax.rsqrt(var + 1e-06)
-
-
-def decode_sides(emb, w_query, w_keyval, w_out, w_head, gains):
-    width = emb.shape[-1]
-    head_size = width // HEADS
-    count = emb.shape[0]
-    tokv = emb.shape[2]
-    records = []
-    for side in range(2):
-        other = 1 - side
-        query_in = (layer_norm(emb[:, side].astype(jnp.float32)) * gains[side, 0]).astype(
-            jnp.bfloat16
-        )
-        memory_in = (layer_norm(emb[:, other].astype(jnp.float32)) * gains[side, 1]).astype(
-            jnp.bfloat16
-        )
-        query = jnp.einsum(
-            "ptd,de->pte", query_in, w_query[side], preferred_element_type=jnp.float32
-        ).astype(jnp.bfloat16)
-        keyval = jnp.einsum(
-            "ptd,de->pte", memory_in, w_keyval[side], preferred_element_type=jnp.float32
-        ).astype(jnp.bfloat16)
-        query_h = query.reshape(count, tokv, HEADS, head_size)
-        key_h = keyval[..., :width].reshape(count, tokv, HEADS, head_size)
-        value_h = keyval[..., width:].reshape(count, tokv, HEADS, head_size)
-        scores = jnp.einsum(
-            "pqhd,pkhd->phqk", query_h, key_h, preferred_element_type=jnp.float32
-        ) * (1.0 / head_size**0.5)
-        probs = jax.nn.softmax(scores, axis=-1).astype(jnp.bfloat16)
-        context = jnp.einsum("phqk,pkhd->pqhd", probs, value_h, preferred_element_type=jnp.float32)
-        context = context.astype(jnp.bfloat16).reshape(count, tokv, width)
-        updated = emb[:, side].astype(jnp.float32) + jnp.einsum(
-            "ptd,de->pte", context, w_out[side], preferred_element_type=jnp.float32
-        )
-        final = (layer_norm(updated) * gains[side, 2]).astype(jnp.bfloat16)
-        head = jnp.einsum("cd,ptd->pct", w_head[side], final, preferred_element_type=jnp.float32)
-        conf = 1.0 + jnp.exp(head[:, 3])
-        records.append(jnp.concatenate([conf[:, None, :] * head[:, :3], conf[:, None, :]], axis=1))
-    return jnp.stack(records, axis=1)
 
 
 NY = 4
@@ -339,47 +293,170 @@
     return wanted, places
 
 
+def normal(values):
+    mean = jnp.mean(values, axis=-1, keepdims=True)
+    centred = values - mean
+    var = jnp.mean(centred * centred, axis=-1, keepdims=True)
+    return centred * lax.rsqrt(var + 1e-06)
+
+
+def decode_kernel(sides, spread, w_query, w_keyval, w_out, w_head, gains, sums, query, keyval, context, out, block, toward, came, mine_sum, every, s1, r1, s2, r2, s3, r3):
+    count, tokv, width = sides.shape
+    nm, nv = out.shape[0], toward.shape[0]
+    view = lax.axis_index("view")
+    me = lax.axis_index("mp")
+    barrier = pltpu.get_barrier_semaphore()
+    columns_peers = [(view, lax.rem(me + o, nm)) for o in range(1, nm)]
+    view_peers = [(lax.rem(view + o, nv), me) for o in range(1, nv)]
+    for peer in columns_peers + view_peers:
+        pl.semaphore_signal(barrier, inc=1, device_id=peer, device_id_type=MESH)
+    size = width // HEADS
+    scale = 1.4426950408889634 / size**0.5
+    f32, bf16 = jnp.float32, jnp.bfloat16
+
+    @pl.loop(0, count)
+    def one_side(i):
+        side = lax.rem(i, 2)
+        gain = gains[side]
+        query_in = (normal(sides[i].astype(f32)) * gain[0:1]).astype(bf16)
+        query[...] = jnp.dot(query_in, w_query[side], preferred_element_type=f32).astype(bf16)
+        memory_in = (normal(sides[i + 1 - 2 * side].astype(f32)) * gain[1:2]).astype(bf16)
+        keyval[...] = jnp.dot(memory_in, w_keyval[side], preferred_element_type=f32).astype(bf16)
+        lane = lax.broadcasted_iota(jnp.int32, (tokv, 2 * size), 1)
+        first = lane < size
+        ones = jnp.ones((tokv, 2 * size), bf16)
+        for h in range(0, HEADS, 2):
+            columns = slice(h * size, (h + 2) * size)
+            both = query[:, columns]
+            keys = keyval[:, columns]
+            values = jnp.concatenate(
+                [keyval[:, width + h * size : width + (h + 2) * size], ones], axis=1
+            )
+            found = []
+            for half in range(2):
+                mine = jnp.where(first if half == 0 else jnp.logical_not(first), both, jnp.zeros_like(both))
+                scores = lax.dot_general(
+                    mine, keys, (((1,), (1,)), ((), ())), preferred_element_type=f32
+                )
+                top = jnp.max(scores, axis=-1, keepdims=True)
+                probs = jnp.exp2((scores - top) * scale).astype(bf16)
+                total = jnp.dot(probs, values, preferred_element_type=f32)
+                found.append(total[:, : 2 * size] / total[:, 2 * size :])
+            context[:, columns] = jnp.where(first, found[0], found[1]).astype(bf16)
+        updated = sides[i].astype(f32) + jnp.dot(
+            context[...], w_out[side], preferred_element_type=f32
+        )
+        final = (normal(updated) * gain[2:3]).astype(bf16)
+        head = lax.dot_general(
+            w_head[side], final, (((1,), (1,)), ((), ())), preferred_element_type=f32
+        )
+        conf = 1.0 + jnp.exp(head[3:4])
+        for c in range(4):
+            record = conf * head[c : c + 1] if c < 3 else conf
+            for b in range(tokv // 128):
+                row = c * (tokv // 128) + b
+                out[row // 2, pl.ds(row % 2 * count + i, 1), :] = record[:, b * 128 : (b + 1) * 128]
+
+    pl.semaphore_wait(barrier, nm + nv - 2)
+    sent, coming = [], []
+
+    def start(copy):
+        copy.start()
+        sent.append(copy)
+        coming.append(copy)
+
+    def arrive():
+        for copy in coming:
+            copy.wait_recv()
+        coming.clear()
+
+    for o in range(1, nm):
+        start(remote(out.at[lax.rem(me + o, nm)], block.at[me], s1.at[o], r1.at[o], columns_peers[o - 1]))
+    block[me] = out[me]
+    arrive()
+    toward[...] = jnp.dot(
+        spread[...],
+        block[...].reshape(nm * 8, 128),
+        precision=lax.Precision.HIGHEST,
+        preferred_element_type=f32,
+    ).reshape(nv, 8, 128)
+    for o in range(1, nv):
+        start(remote(toward.at[lax.rem(view + o, nv)], came.at[view], s2.at[o], r2.at[o], view_peers[o - 1]))
+    came[view] = toward[view]
+    arrive()
+    mine_sum[...] = jnp.sum(came[...], axis=0)
+    for o in range(1, nm):
+        start(remote(mine_sum, every.at[me], s3.at[o], r3.at[o], columns_peers[o - 1]))
+    every[me] = mine_sum[...]
+    arrive()
+    blocks = tokv // 128
+    for local in range(sums.shape[0]):
+        for row in range(4 * blocks):
+            place = row % blocks * 128
+            sums[local, row // blocks, place : place + 128] = every[row // 2, local * 2 + row % 2]
+    for copy in sent:
+        copy.wait_send()
+
+
+def plan_spread(side_views, views, view_dev, nm):
+    count = side_views.shape[0] // nm
+    column = jnp.arange(nm * 2 * count, dtype=jnp.int32)
+    row = jnp.arange(views * 2, dtype=jnp.int32)
+    column_view = jnp.broadcast_to(side_views.reshape(nm, 1, count), (nm, 2, count)).reshape(-1)
+    same = jnp.logical_and(
+        row[:, None] // 2 == column_view[None, :], row[:, None] % 2 == (column // count % 2)[None, :]
+    )
+    return same.astype(jnp.float32)
+
+
+def decode(sides, spread, w_query, w_keyval, w_out, w_head, gains):
+    count, tokv, width = sides.shape
+    nm = lax.axis_size("mp")
+    nv = lax.axis_size("view")
+    view_dev = spread.shape[0] // (2 * nv)
+    vmem = pl.BlockSpec(memory_space=pltpu.VMEM)
+    dma = pltpu.SemaphoreType.DMA
+    f32 = jnp.float32
+    pad = lambda a: jnp.pad(a, ((0, 0), (0, 8 - a.shape[1]), (0, 0)))
+    return pl.pallas_call(
+        decode_kernel,
+        out_shape=jax.ShapeDtypeStruct((view_dev, 4, tokv), f32),
+        in_specs=[vmem] * 7,
+        out_specs=vmem,
+        scratch_shapes=[
+            pltpu.VMEM((tokv, width), jnp.bfloat16),
+            pltpu.VMEM((tokv, 2 * width), jnp.bfloat16),
+            pltpu.VMEM((tokv, width), jnp.bfloat16),
+            pltpu.VMEM((nm, 8, 128), f32),
+            pltpu.VMEM((nm, 8, 128), f32),
+            pltpu.VMEM((nv, 8, 128), f32),
+            pltpu.VMEM((nv, 8, 128), f32),
+            pltpu.VMEM((8, 128), f32),
+            pltpu.VMEM((nm, 8, 128), f32),
+            dma((nm,)),
+            dma((nm,)),
+            dma((nv,)),
+            dma((nv,)),
+            dma((nm,)),
+            dma((nm,)),
+        ],
+        compiler_params=pltpu.CompilerParams(
+            collective_id=1, has_side_effects=True, vmem_limit_bytes=52 * 2**20
+        ),
+    )(sides, spread, w_query, w_keyval, w_out, pad(w_head), pad(gains))
+
+
 def on_device(tokens, pairs, w_embed, w_query, w_keyval, w_out, w_head, gains):
     view_count = lax.axis_size("view")
     column_count = lax.axis_size("mp")
-    me = lax.axis_index("view")
-    view_dev, tokv, unused = tokens.shape
-    block_pairs = pairs.shape[0]
-    pair_dev = block_pairs // column_count
-    side_count = 2 * block_pairs
+    view_dev = tokens.shape[0]
+    side_count = 2 * pairs.shape[0]
     cap = max(2, (side_count + view_count - 1) // view_count)
-    all_pairs = lax.all_gather(pairs, "view", axis=0, tiled=True)
     side_views = pairs.reshape(side_count)
     wanted, places = plan_sides(side_views, view_dev, cap)
-    sides = gather_sides(tokens, wanted, places, w_embed).reshape(pair_dev, 2, tokv, -1)
-    results = decode_sides(sides, w_query, w_keyval, w_out, w_head, gains)
-
-    chunk = 4 * tokv // column_count
-    shares = results.reshape(2 * pair_dev, column_count, chunk)
-    shares = lax.all_to_all(shares, "mp", split_axis=1, concat_axis=0, tiled=False)
-    shares = shares.reshape(side_count, chunk)
-    owners = side_views // view_dev
-    positions = jnp.arange(side_count, dtype=jnp.int32)
-    earlier = jnp.logical_and(
-        owners[:, None] == owners[None, :], positions[None, :] < positions[:, None]
-    )
-    slot_index = owners * cap + jnp.sum(earlier, axis=1)
-    match = jnp.arange(view_count * cap, dtype=jnp.int32)[:, None] == slot_index[None, :]
-    outgoing = jnp.sum(jnp.where(match[..., None], shares[None], 0.0), axis=1).reshape(view_count, cap, chunk)
-    incoming = lax.all_to_all(outgoing, "view", split_axis=0, concat_axis=0, tiled=True)
-
-    asked = all_pairs.reshape(view_count, side_count)
-    mine = asked // view_dev == me
-    rank = jnp.sum(
-        jnp.logical_and(mine[:, None, :], positions[None, None, :] < positions[None, :, None]), axis=2
-    )
-    slot = jnp.arange(cap, dtype=jnp.int32)
-    hit = jnp.logical_and(mine[:, None, :], rank[:, None, :] == slot[None, :, None])
-    local = jnp.sum(jnp.where(hit, (asked % view_dev + 1)[:, None, :], 0), axis=2) - 1
-    picks = local[None] == jnp.arange(view_dev, dtype=jnp.int32)[:, None, None]
-    owned = jnp.sum(jnp.where(picks[..., None], incoming[None], 0.0), axis=(1, 2))
-    gathered = lax.all_gather(owned, "mp", axis=1, tiled=True)
-    return gathered.reshape(view_dev, 4, tokv)
+    spread = plan_spread(side_views, view_count * view_dev, view_dev, column_count)
+    sides = gather_sides(tokens, wanted, places, w_embed)
+    return decode(sides, spread, w_query, w_keyval, w_out, w_head, gains)
 
 
 def solution(mesh):

time: 237 us -> 138 us (0.58)
  blocking collectives: 57.3 us -> 0 us
  matrix products: 47.7 us -> 0 us
  Pallas kernels: 86.2 us -> 130 us
  local copies, waits for them, and re-layouts: 23.9 us -> 6.88 us
  waiting for transfers between devices: 8.81 us -> 0 us
  starting transfers between devices: 7.54 us -> 0 us
  other arithmetic: 3.91 us -> 0.45 us
    all_gather x2 -> x0, blocking collectives: 57.3 us -> none  [the longest x1 32.9 us: on_device(): all_pairs = lax.all_gather(pairs, 'view', axis=0, tiled=True)]
    pallas_call x0 -> x1, Pallas kernels: none -> 44.1 us  [decode(): pl.pallas_call(decode_kernel, out_shape=jax.ShapeDtypeStruct((view_dev, 4...]
    dot_general x10 -> x0, matrix products: 29.2 us -> none  [the longest x2 12.8 us: decode_sides(): jnp.einsum('phqk,pkhd->pqhd', probs, value_h, preferred_element_type=jnp....]
    sub x2 -> x0, matrix products: 18.5 us -> none  [decode_sides(): probs = jax.nn.softmax(scores, axis=-1).astype(jnp.bfloat16)]
    slice x7 -> x0, local copies, waits for them, and re-layouts: 11.3 us -> none  [the longest x4 5.14 us: decode_sides(): key_h = keyval[..., :width].reshape(count, tokv, HEADS, head_size)]
    all_to_all x2 -> x0, waiting for transfers between devices: 8.81 us -> none  [the longest x1 8.81 us: on_device(): lax.all_to_all(outgoing, 'view', split_axis=0, concat_axis=0, tiled=True)]
    all_to_all x2 -> x0, starting transfers between devices: 7.54 us -> none  [the longest x1 4.26 us: on_device(): lax.all_to_all(outgoing, 'view', split_axis=0, concat_axis=0, tiled=True)]
    convert_element_type x2 -> x0, local copies, waits for them, and re-layouts: 4.8 us -> none  [decode_sides(): query = jnp.einsum('ptd,de->pte', query_in, w_query[side], preferred_elem...]
  transfers between devices with their start and end apart: 2 -> 0, of which waited for: 1 -> 0; matrix products, arithmetic and copies ran while one was open for 0% -> 0% of each run, Pallas kernels for 0% -> 0%
where the time goes in v3:
time: 138 us
  Pallas kernels  130 us (94%)
  local copies, waits for them, and re-layouts  6.88 us (5%)
    pallas_call x1, Pallas kernels, gather_sides(): pl.pallas_call(functools.partial(gather_kernel, nz, nm, chunks), out_shap...  86.2 us
    pallas_call x1, Pallas kernels, decode(): pl.pallas_call(decode_kernel, out_shape=jax.ShapeDtypeStruct((view_dev, 4...  44.1 us
    unnamed x9, local copies, waits for them, and re-layouts  5.9 us

profile of v3, /device:TPU:1, one launch (start us, length us, event | category | flops | bytes accessed | tf_op | source)
XLA Modules:
  0.0 137.7 jit_solution(17908999065835090452)
XLA Ops:
  0.0 0.8 copy.18
  0.8 0.1 reshape.172
  0.9 0.1 broadcast_in_dim.21
  0.9 0.2 convert_reduce_fusion
  1.2 0.1 select_reduce_fusion
  1.3 0.1 eq.86
  1.4 0.7 pad.8.w_head
  2.1 0.7 copy.21
  2.8 0.1 and_convert_fusion.spread
  3.0 0.0 copy-start.1
  3.0 1.4 %copy-done.1 = bf16[1024,768]{1,0:T(8,128)(2,1)S(1)} copy-done((bf16[1024,768]{1,0:T(8,128)(2,1)S(1)}, bf16[1024,768]{1,0:T(8,128)(2,1)}, u32[]{:S(2)}) %copy-start.1) | copy-done | bytes 1572888
  4.4 0.0 copy-start.2
  4.4 1.0 copy-done.2
  5.4 86.2 %shard_map.82.sides = bf16[4,384,768]{2,1,0:T(8,128)(2,1)S(1)} custom-call(bf16[4,384,128]{2,1,0:T(8,128)(2,1)S(1)} %copy-done.2, s32[8,128]{1,0:T(8,128)S(1)} %broadcast_in_dim.20.wanted, s32[32]{0:T(128)S(1)} %get-tuple-element.5.places, bf16[1024,768]{1,0:T(8,128)(2,1)S(1)} %copy-done.1), custom_call_target="tpu_custom_call" | custom-call | tf_op jit(solution)/shard_map/pallas_call | solution.py:241
  91.6 0.0 copy-start
  91.6 1.4 %copy-done = bf16[4,384,768]{2,1,0:T(8,128)(2,1)} copy-done((bf16[4,384,768]{2,1,0:T(8,128)(2,1)}, bf16[4,384,768]{2,1,0:T(8,128)(2,1)S(1)}, u32[]{:S(2)}) %copy-start) | copy-done | bytes 2359320
  93.0 44.1 %shard_map.83 = f32[4,4,384]{2,1,0:T(4,128)S(1)} custom-call(bf16[4,384,768]{2,1,0:T(8,128)(2,1)} %copy-done, f32[256,64]{1,0:T(8,128)S(1)} %and_convert_fusion.spread, bf16[2,768,768]{2,1,0:T(8,128)(2,1)} %w_query.1, bf16[2,768,1536]{2,1,0:T(8,128)(2,1)} %w_keyval.1, bf16[2,768,768]{2,1,0:T(8,128)(2,1)} %w_out.1, bf16[2,8,768]{2,1,0:T(8,128)(2,1)S(1)} %pad.8.w_head, ...), custom_call_target="tpu_custom_call" | custom-call | tf_op jit(solution)/shard_map/pallas_call | solution.py:421
  137.0 0.6 copy.23
  (7 shorter events, 0.1 us)
Async XLA Ops:
  3.0 1.4 %copy-start.1 = (bf16[1024,768]{1,0:T(8,128)(2,1)S(1)}, bf16[1024,768]{1,0:T(8,128)(2,1)}, u32[]{:S(2)}) copy-start(bf16[1024,768]{1,0:T(8,128)(2,1)} %w_embed.1) | copy-start | bytes 4718596
  4.4 1.0 copy-start.2
  91.6 1.4 %copy-start = (bf16[4,384,768]{2,1,0:T(8,128)(2,1)}, bf16[4,384,768]{2,1,0:T(8,128)(2,1)S(1)}, u32[]{:S(2)}) copy-start(bf16[4,384,768]{2,1,0:T(8,128)(2,1)S(1)} %shard_map.82.sides) | copy-start | bytes 7077892

commit v4 on v0

v4 whole, which is shorter than its diff:
```python
import functools

import jax
import jax.numpy as jnp
from jax import lax
from jax.experimental import pallas as pl
from jax.experimental.pallas import tpu as pltpu
from jax.sharding import PartitionSpec as P

HEADS = 12
NY = 4
ROWS = 16
MESH = pl.DeviceIdType.MESH
FAR = (False, True, True)
STEPS = (3.0, 4.0)
SHIFT = (7.0, 13.0)
SLOTS = (2.2, 1.1)
X_LAG = 5.0


def normal(values):
    mean = jnp.mean(values, axis=-1, keepdims=True)
    centred = values - mean
    var = jnp.mean(centred * centred, axis=-1, keepdims=True)
    return centred * lax.rsqrt(var + 1e-06)


def remote(source, target, send, arrive, device):
    return pltpu.make_async_remote_copy(
        src_ref=source,
        dst_ref=target,
        send_sem=send,
        recv_sem=arrive,
        device_id=device,
        device_id_type=MESH,
    )


def offsets(nz, c, t):
    up = nz // 2 if c % 2 == 0 else (nz - 1) // 2
    down = nz - 1 - up
    if t == 0:
        return [(0, (1,) * (up > 0) + (-1,) * (down > 0))]
    found = []
    if t <= up:
        found.append((nz - t, (1,) * (t < up)))
    if t <= down:
        found.append((t, (-1,) * (t < down)))
    return found


def schedule(nz, chunks):
    events = []
    y_free = begin = 0.0
    for c in range(chunks):
        far = FAR[c]
        last = 0.0
        for t in range(nz // 2 + 1):
            now = begin + t * STEPS[far]
            events.append((now, "near", c, t))
            if far:
                last = now + STEPS[far]
                events.append((last, "far", c, t))
            y_free = max(y_free, now)
            events.append((y_free, "slots", c, t))
            y_free += len(offsets(nz, c, t)) * SLOTS[far]
        begin += SHIFT[far]
        events.append((max(last, y_free + X_LAG), "hand", c, 0))
    rank = {"near": 0, "far": 1, "slots": 2, "hand": 3}
    return sorted(events, key=lambda e: (e[0], rank[e[1]], e[2], e[3]))


def project(c, sides, w_query, w_keyval, gains, query, keyval):
    chunks, count, rows, width = sides.shape
    f32, bf16 = jnp.float32, jnp.bfloat16
    pairs = count // 2
    for side in range(2):
        views = jnp.concatenate([sides[c, 2 * p + side] for p in range(pairs)], axis=0)
        level = normal(views.astype(f32))
        query_in = (level * gains[side, 0:1]).astype(bf16)
        found = jnp.dot(query_in, w_query[side], preferred_element_type=f32).astype(bf16)
        for p in range(pairs):
            query[2 * p + side, c * rows : (c + 1) * rows] = found[p * rows : (p + 1) * rows]
        memory_in = (level * gains[1 - side, 1:2]).astype(bf16)
        found = jnp.dot(memory_in, w_keyval[1 - side], preferred_element_type=f32).astype(bf16)
        for p in range(pairs):
            keyval[2 * p + 1 - side, c * rows : (c + 1) * rows] = found[p * rows : (p + 1) * rows]


def attend(i, sides, w_out, w_head, gains, query, keyval, context, ordered, out):
    chunks, count, rows, width = sides.shape
    tokv = chunks * rows
    size = width // HEADS
    scale = 1.4426950408889634 / size**0.5
    f32, bf16 = jnp.float32, jnp.bfloat16
    side = lax.rem(i, 2)
    gain = gains[side]
    lane = lax.broadcasted_iota(jnp.int32, (tokv, 2 * size), 1)
    first = lane < size
    ones = jnp.ones((tokv, 2 * size), bf16)
    for h in range(0, HEADS, 2):
        columns = slice(h * size, (h + 2) * size)
        both = query[i, :, columns]
        keys = keyval[i, :, columns]
        values = jnp.concatenate(
            [keyval[i, :, width + h * size : width + (h + 2) * size], ones], axis=1
        )
        found = []
        for half in range(2):
            mine = jnp.where(first if half == 0 else jnp.logical_not(first), both, jnp.zeros_like(both))
            scores = lax.dot_general(
                mine, keys, (((1,), (1,)), ((), ())), preferred_element_type=f32
            )
            top = jnp.max(scores, axis=-1, keepdims=True)
            probs = jnp.exp2((scores - top) * scale).astype(bf16)
            total = jnp.dot(probs, values, preferred_element_type=f32)
            found.append(total[:, : 2 * size] / total[:, 2 * size :])
        context[:, columns] = jnp.where(first, found[0], found[1]).astype(bf16)
    emb = jnp.concatenate([sides[c, i] for c in range(chunks)], axis=0)
    updated = emb.astype(f32) + jnp.dot(context[...], w_out[side], preferred_element_type=f32)
    final = (normal(updated) * gain[2:3]).astype(bf16)
    parts = rows // ROWS
    for c in range(chunks):
        for j in range(parts):
            place = (j * chunks + c) * ROWS
            come = (c * parts + j) * ROWS
            ordered[place : place + ROWS] = final[come : come + ROWS]
    head = lax.dot_general(
        w_head[side], ordered[...], (((1,), (1,)), ((), ())), preferred_element_type=f32
    )
    conf = 1.0 + jnp.exp(head[3:4])
    for c in range(4):
        record = conf * head[c : c + 1] if c < 3 else conf
        for b in range(tokv // 128):
            row = c * (tokv // 128) + b
            out[row // 2, pl.ds(row % 2 * count + i, 1), :] = record[:, b * 128 : (b + 1) * 128]


def kernel(nz, nm, chunks, *refs):
    refs = iter(refs)

    def take(n):
        return [next(refs) for unused in range(n)]

    tokens, wanted, places, spread, w_head, gains = take(6)
    in_hbm = take(4)
    (sums,) = take(1)
    w_embed, w_query, w_keyval, w_out = in_vmem = take(4)
    full, w_near, w_held, slots, parcels, sides = take(6)
    query, keyval, context, ordered, out, block, toward, came, mine_sum, every = take(10)
    pools = take(chunks)
    held = [take(nz) for unused in range(chunks)]
    distant = [take(nz) for unused in range(chunks)]
    (local, s1, r1, s2, r2, s3, r3, t_send, t_recv, w_send, w_recv) = take(11)
    (z_send, z_recv, p_send, p_recv, y_send, y_recv, x_send, x_recv) = take(8)

    view = lax.axis_index("view")
    me = lax.axis_index("mp")
    z = view // NY
    y = view % NY
    nv = nz * NY
    part = tokens.shape[1] // nm
    feat = tokens.shape[2]
    view_dev = tokens.shape[0]
    count = places.shape[0] // nm
    tokv = tokens.shape[1]

    def at_z(step):
        return (lax.rem(z + step + nz, nz) * NY + y, me)

    def at_y(step):
        return (z * NY + lax.rem(y + step + NY, NY), me)

    column_peers = [(view, lax.rem(me + o, nm)) for o in range(1, nm)]
    view_peers = [(lax.rem(view + o, nv), me) for o in range(1, nv)]
    barrier = pltpu.get_barrier_semaphore()
    for peer in column_peers + view_peers:
        pl.semaphore_signal(barrier, inc=1, device_id=peer, device_id_type=MESH)
    loads = [pltpu.make_async_copy(a, b, local.at[k]) for k, (a, b) in enumerate(zip(in_hbm, in_vmem))]
    loads[0].start()
    own = pltpu.make_async_copy(
        tokens.at[:, pl.ds(pl.multiple_of(me * part, ROWS), part), :],
        full.at[:, :, pl.ds(pl.multiple_of(me * feat, 128), feat)],
        local.at[4],
    )
    own.start()
    own_wanted = pltpu.make_async_copy(wanted, w_near.at[0], local.at[5])
    own_wanted.start()
    pl.semaphore_wait(barrier, nm + nv - 2)

    sent = []

    def start(copy):
        copy.start()
        sent.append(copy)
        return copy

    def receive(copies):
        for copy in copies:
            copy.wait_recv()

    arriving = []
    for o in range(1, nm):
        j = lax.rem(me + o, nm)
        arriving.append(
            start(
                remote(
                    tokens.at[:, pl.ds(pl.multiple_of(j * part, ROWS), part), :],
                    full.at[:, :, pl.ds(pl.multiple_of(me * feat, 128), feat)],
                    t_send.at[o],
                    t_recv.at[o],
                    column_peers[o - 1],
                )
            )
        )
    asking = [
        start(remote(wanted, w_near.at[NY - o], w_send.at[o], w_recv.at[NY - o], at_y(o)))
        for o in range(1, NY)
    ]
    for load in loads[1:]:
        load.start()
    own.wait()
    loads[0].wait()
    receive(arriving)
    emb = jnp.dot(
        full[...].reshape(view_dev * part, nm * feat), w_embed[...], preferred_element_type=jnp.float32
    )
    emb = emb.astype(jnp.bfloat16).reshape(view_dev, part, -1)
    for c in range(chunks):
        held[c][0][...] = emb[:, c * ROWS : (c + 1) * ROWS]

    z_copy, y_copy, x_copy, p_copy = {}, {}, {}, {}
    first_slot = [lax.rem(z + d, nz) * (NY * 2) for d in range(nz)]
    column_slot = [lax.rem(y + dy, NY) * 2 for dy in range(NY)]

    def choose(table, c, d, dy, dest, r):
        return table[c][d][w_held[dest, 0, first_slot[d] + column_slot[dy] + r]]

    def move(kind, table, c, d, ways):
        for way in ways:
            target = (d - way) % nz
            z_copy[kind, c, target] = start(
                remote(
                    table[c][d],
                    table[c][target],
                    z_send.at[c, kind, target],
                    z_recv.at[c, kind, target],
                    at_z(way),
                )
            )

    def near(c, t):
        for d, ways in offsets(nz, c, t):
            if t:
                z_copy[0, c, d].wait_recv()
            move(0, held, c, d, ways)
            if t == 0 and FAR[c]:
                p_copy[c] = start(remote(held[c][0], distant[c][0], p_send.at[c], p_recv.at[c], at_y(2)))

    def far(c, t):
        for d, ways in offsets(nz, c, t):
            (z_copy[1, c, d] if t else p_copy[c]).wait_recv()
            move(1, distant, c, d, ways)
        for d, ways in offsets(nz, c, t):
            for r in range(2):
                pools[c][4 * nz + 2 * d + r] = choose(distant, c, d, 2, 0, r)

    def send_slots(c, t):
        for d, unused in offsets(nz, c, t):
            for way, dest in enumerate((1, 3) if FAR[c] else (1, 3, 2)):
                for r in range(2):
                    slots[c, way, d, r] = choose(held, c, d, 0, dest, r)
                y_copy[c, way, d] = start(
                    remote(
                        slots.at[c, way, d],
                        pools[c].at[pl.ds(2 * nz * way + 2 * d, 2)],
                        y_send.at[c, way, d],
                        y_recv.at[c, way, d],
                        at_y(dest),
                    )
                )
            for r in range(2):
                pools[c][6 * nz + 2 * d + r] = choose(held, c, d, 0, 0, r)

    def hand(c, unused):
        receive([copy for key, copy in y_copy.items() if key[0] == c])
        rows = pl.ds(pl.multiple_of(me * ROWS, ROWS), ROWS)
        for o in range(1, nm):
            j = lax.rem(me + o, nm)
            for k in range(count):
                parcels[c, o, k] = pools[c][places[j * count + k]]
            x_copy[c, o] = start(
                remote(
                    parcels.at[c, o],
                    sides.at[c, :, rows, :],
                    x_send.at[c, o],
                    x_recv.at[c, o],
                    column_peers[o - 1],
                )
            )
        for k in range(count):
            sides[c, k, rows, :] = pools[c][places[me * count + k]]

    acts = {"near": near, "far": far, "slots": send_slots, "hand": hand}
    asked = False
    for unused, kind, c, t in schedule(nz, chunks):
        if not asked and kind in ("slots", "far"):
            asked = True
            own_wanted.wait()
            receive(asking)
            to_scalars = pltpu.make_async_copy(w_near, w_held, local.at[6])
            to_scalars.start()
            to_scalars.wait()
        acts[kind](c, t)
    for load in loads[1:]:
        load.wait()
    for c in range(chunks):
        receive([x_copy[c, o] for o in range(1, nm)])
        project(c, sides, w_query, w_keyval, gains, query, keyval)

    @pl.loop(0, count)
    def one_side(i):
        attend(i, sides, w_out, w_head, gains, query, keyval, context, ordered, out)

    receive(
        [
            start(remote(out.at[lax.rem(me + o, nm)], block.at[me], s1.at[o], r1.at[o], column_peers[o - 1]))
            for o in range(1, nm)
        ]
        + []
    )
    block[me] = out[me]
    toward[...] = jnp.dot(
        spread[...],
        block[...].reshape(nm * 8, 128),
        precision=lax.Precision.HIGHEST,
        preferred_element_type=jnp.float32,
    ).reshape(nv, 8, 128)
    came[view] = toward[view]
    receive(
        [
            start(remote(toward.at[lax.rem(view + o, nv)], came.at[view], s2.at[o], r2.at[o], view_peers[o - 1]))
            for o in range(1, nv)
        ]
    )
    mine_sum[...] = jnp.sum(came[...], axis=0)
    every[me] = mine_sum[...]
    receive(
        [
            start(remote(mine_sum, every.at[me], s3.at[o], r3.at[o], column_peers[o - 1]))
            for o in range(1, nm)
        ]
    )
    blocks = tokv // 128
    for index in range(view_dev):
        for row in range(4 * blocks):
            place = row % blocks * 128
            sums[index, row // blocks, place : place + 128] = every[row // 2, index * 2 + row % 2]
    for copy in sent:
        copy.wait_send()


def plan_sides(side_views, view_dev, cap):
    view_count = lax.axis_size("view")
    nz = view_count // NY
    me = lax.axis_index("view")
    count = side_views.shape[0]
    owners = side_views // view_dev
    positions = jnp.arange(count, dtype=jnp.int32)
    earlier = jnp.logical_and(
        owners[:, None] == owners[None, :], positions[None, :] < positions[:, None]
    )
    rank = jnp.sum(earlier, axis=1)
    slot_index = owners * cap + rank
    match = jnp.arange(128, dtype=jnp.int32)[:, None] == slot_index[None, :]
    wanted = jnp.sum(jnp.where(match, (side_views % view_dev)[None, :], 0), axis=1)
    wanted = jnp.broadcast_to(wanted[None, :], (8, 128))
    d = (owners // NY - me // NY + nz) % nz
    rel = (owners % NY - me % NY + NY) % NY
    base = jnp.where(rel == 0, 3, jnp.where(rel == 3, 0, jnp.where(rel == 1, 1, 2)))
    places = base * (2 * nz) + 2 * d + rank
    return wanted, places


def plan_spread(side_views, views, view_dev, nm):
    count = side_views.shape[0] // nm
    column = jnp.arange(nm * 2 * count, dtype=jnp.int32)
    row = jnp.arange(views * 2, dtype=jnp.int32)
    column_view = jnp.broadcast_to(side_views.reshape(nm, 1, count), (nm, 2, count)).reshape(-1)
    same = jnp.logical_and(
        row[:, None] // 2 == column_view[None, :], row[:, None] % 2 == (column // count % 2)[None, :]
    )
    return same.astype(jnp.float32)


def on_device(tokens, pairs, w_embed, w_query, w_keyval, w_out, w_head, gains):
    nv = lax.axis_size("view")
    nm = lax.axis_size("mp")
    nz = nv // NY
    view_dev, tokv, feat = tokens.shape
    width = w_embed.shape[1]
    sides_all = 2 * pairs.shape[0]
    count = sides_all // nm
    side_views = pairs.reshape(sides_all)
    wanted, places = plan_sides(side_views, view_dev, 2)
    spread = plan_spread(side_views, nv * view_dev, view_dev, nm)
    part = tokv // nm
    chunks = part // ROWS
    piece = (ROWS, width)
    f32, bf16, i32 = jnp.float32, jnp.bfloat16, jnp.int32
    vmem = pl.BlockSpec(memory_space=pltpu.VMEM)
    hbm = pl.BlockSpec(memory_space=pltpu.HBM)
    dma = pltpu.SemaphoreType.DMA
    weights = (w_embed, w_query, w_keyval, w_out)
    return pl.pallas_call(
        functools.partial(kernel, nz, nm, chunks),
        out_shape=jax.ShapeDtypeStruct((view_dev, 4, tokv), f32),
        in_specs=[hbm, vmem, pl.BlockSpec(memory_space=pltpu.SMEM), vmem, vmem, vmem] + [hbm] * 4,
        out_specs=vmem,
        scratch_shapes=[pltpu.VMEM(w.shape, bf16) for w in weights]
        + [
            pltpu.VMEM((view_dev, part, nm * feat), bf16),
            pltpu.VMEM((NY,) + wanted.shape, i32),
            pltpu.SMEM((NY,) + wanted.shape, i32),
            pltpu.VMEM((chunks, 3, nz, 2) + piece, bf16),
            pltpu.VMEM((chunks, nm, count) + piece, bf16),
            pltpu.VMEM((chunks, count, nm * ROWS, width), bf16),
            pltpu.VMEM((count, tokv, width), bf16),
            pltpu.VMEM((count, tokv, 2 * width), bf16),
            pltpu.VMEM((tokv, width), bf16),
            pltpu.VMEM((tokv, width), bf16),
            pltpu.VMEM((nm, 8, 128), f32),
            pltpu.VMEM((nm, 8, 128), f32),
            pltpu.VMEM((nv, 8, 128), f32),
            pltpu.VMEM((nv, 8, 128), f32),
            pltpu.VMEM((8, 128), f32),
            pltpu.VMEM((nm, 8, 128), f32),
        ]
        + [pltpu.VMEM((8 * nz,) + piece, bf16)] * chunks
        + [pltpu.VMEM((view_dev,) + piece, bf16)] * (2 * chunks * nz)
        + [dma((7,))]
        + [dma((nm,))] * 2
        + [dma((nv,))] * 2
        + [dma((nm,))] * 4
        + [dma((NY,))] * 2
        + [dma((chunks, 2, nz))] * 2
        + [dma((chunks,))] * 2
        + [dma((chunks, 3, nz))] * 2
        + [dma((chunks, nm))] * 2,
        compiler_params=pltpu.CompilerParams(
            collective_id=0, has_side_effects=True, vmem_limit_bytes=60 * 2**20
        ),
    )(tokens, wanted, places, spread, w_head, gains, *weights)


def solution(mesh):
    return jax.shard_map(
        on_device,
        mesh=mesh,
        in_specs=(P("view", None, "mp"), P("view", None), P(), P(), P(), P(), P(), P()),
        out_specs=P("view", None, None),
        check_vma=False,
    )
```

time: 475 us -> 123 us (0.26)
  waiting for transfers between devices: 311 us -> 0 us
  Pallas kernels: 0 us -> 116 us
  matrix products: 51.4 us -> 0 us
  blocking collectives: 45.8 us -> 0 us
  local copies, waits for them, and re-layouts: 29.2 us -> 4.29 us
  starting transfers between devices: 15.3 us -> 0 us
  between operations: 14.4 us -> 0.03 us
  other arithmetic: 6.52 us -> 1.63 us
    all_to_all x2 -> x0, waiting for transfers between devices: 173 us -> none  [the longest x1 135 us: on_device(): lax.all_to_all(payload, 'view', split_axis=0, concat_axis=0, tiled=True)]
    unnamed x2 -> x0, waiting for transfers between devices: 138 us -> none
    pallas_call x0 -> x1, Pallas kernels: none -> 116 us  [on_device(): pl.pallas_call(functools.partial(kernel, nz, nm, chunks), out_shape=jax.S...]
    dot_general x13 -> x0, matrix products: 34.5 us -> none  [the longest x2 12.8 us: decode_sides(): jnp.einsum('phqk,pkhd->pqhd', probs, value_h, preferred_element_type=jnp....]
    psum x1 -> x0, blocking collectives: 25.4 us -> none  [on_device(): return lax.psum(owned, 'mp')]
    all_to_all x1 -> x0, blocking collectives: 20.4 us -> none  [on_device(): lax.all_to_all(wanted, 'view', split_axis=0, concat_axis=0, tiled=True)]
    sub x2 -> x0, matrix products: 16.9 us -> none  [decode_sides(): probs = jax.nn.softmax(scores, axis=-1).astype(jnp.bfloat16)]
    all_to_all x2 -> x0, starting transfers between devices: 15.3 us -> none  [the longest x1 10.3 us: on_device(): lax.all_to_all(parcel, 'mp', split_axis=0, concat_axis=4, tiled=True)]
  transfers between devices with their start and end apart: 3 -> 0, of which waited for: 3 -> 0; matrix products, arithmetic and copies ran while one was open for 0% -> 0% of each run, Pallas kernels for 0% -> 0%
where the time goes in v4:
time: 123 us; the launch traced here: 122 us
  Pallas kernels  116 us (94%)
  local copies, waits for them, and re-layouts  4.29 us (3%)
  other arithmetic  1.63 us (1%)
    pallas_call x1, Pallas kernels, on_device(): pl.pallas_call(functools.partial(kernel, nz, nm, chunks), out_shape=jax.S...  116 us
    unnamed x3, local copies, waits for them, and re-layouts  3.45 us

profile of v4, /device:TPU:1, one launch (start us, length us, event | category | flops | bytes accessed | tf_op | source)
XLA Modules:
  0.0 122.4 jit_solution(3115456727187616460)
XLA Ops:
  0.0 0.8 copy.18
  0.8 0.1 reshape.172
  0.9 0.1 broadcast_in_dim.28
  0.9 0.2 convert_reduce_fusion
  1.1 0.6 fusion.7
  1.7 0.1 select_reduce_fusion
  1.8 0.6 broadcast_in_dim.27.refs_1_
  2.4 0.1 eq.87
  2.5 1.3 %copy.21.refs_5_ = f32[2,3,768]{2,1,0:T(4,128)} copy(f32[2,3,768]{2,0,1:T(2,128)} %param.15) | data formatting | bytes 36864 | tf_op args[7]
  3.8 0.8 and_convert_fusion.refs_3_
  4.6 116.5 %shard_map.82 = f32[4,4,384]{2,1,0:T(4,128)} custom-call(bf16[4,384,128]{2,1,0:T(8,128)(2,1)} %refs_0_.1, s32[8,128]{1,0:T(8,128)} %broadcast_in_dim.27.refs_1_, s32[32]{0:T(128)} %get-tuple-element.5.refs_2_, f32[256,64]{1,0:T(8,128)} %and_convert_fusion.refs_3_, bf16[2,4,768]{2,1,0:T(4,128)(2,1)} %refs_4_.1, f32[2,3,768]{2,1,0:T(4,128)} %copy.21.refs_5_, ...), custom_call_target="tpu_custom_call" | custom-call | tf_op jit(solution)/shard_map/pallas_call | solution.py:415
  121.1 1.3 %copy.23 = f32[4,4,384]{2,1,0:T(4,128)} copy(f32[4,4,384]{2,1,0:T(4,128)} %shard_map.82) | data formatting | bytes 49152
  (4 shorter events, 0.0 us)

commit v5 on v4

v5 whole, which is shorter than its diff:
```python
import functools

import jax
import jax.numpy as jnp
from jax import lax
from jax.experimental import pallas as pl
from jax.experimental.pallas import tpu as pltpu
from jax.sharding import PartitionSpec as P

HEADS = 12
NY = 4
ROWS = 16
MESH = pl.DeviceIdType.MESH
FAR = (False, True, True)
ORDER = (
    (0, 0, 0),
    (0, 0, 1),
    (0, 1, 0),
    (0, 0, 2),
    (1, 0, 1),
    (1, 1, 0),
    (0, 1, 1),
    (0, 0, 3),
    (1, 0, 0),
    (1, 0, 2),
    (0, 1, 2),
    (1, 0, 3),
    (0, 0, 4),
    (0, 2, 0),
    (1, 0, 4),
    (0, 1, 3),
    (1, 1, 2),
    (1, 2, 0),
    (0, 2, 1),
    (1, 1, 3),
    (2, 0, 0),
    (1, 1, 1),
    (0, 1, 4),
    (1, 1, 4),
    (1, 2, 1),
    (0, 2, 2),
    (1, 2, 2),
    (2, 1, 0),
    (0, 2, 3),
    (1, 2, 3),
    (0, 2, 4),
    (1, 2, 4),
    (2, 2, 0),
)


def normal(values):
    mean = jnp.mean(values, axis=-1, keepdims=True)
    centred = values - mean
    var = jnp.mean(centred * centred, axis=-1, keepdims=True)
    return centred * lax.rsqrt(var + 1e-06)


def remote(source, target, send, arrive, device):
    return pltpu.make_async_remote_copy(
        src_ref=source,
        dst_ref=target,
        send_sem=send,
        recv_sem=arrive,
        device_id=device,
        device_id_type=MESH,
    )


def offsets(nz, c, t):
    up = nz // 2 if c % 2 == 0 else (nz - 1) // 2
    down = nz - 1 - up
    if t == 0:
        return [(0, (1,) * (up > 0) + (-1,) * (down > 0))]
    found = []
    if t <= up:
        found.append((nz - t, (1,) * (t < up)))
    if t <= down:
        found.append((t, (-1,) * (t < down)))
    return found


def position(nz, d):
    return 0 if d == 0 else 2 * d if d < nz - d else 2 * (nz - d) - 1


def project(c, sides, w_query, w_keyval, gains, query, keyval):
    chunks, count, rows, width = sides.shape
    f32, bf16 = jnp.float32, jnp.bfloat16
    pairs = count // 2
    for side in range(2):
        views = jnp.concatenate([sides[c, 2 * p + side] for p in range(pairs)], axis=0)
        level = normal(views.astype(f32))
        query_in = (level * gains[0, side : side + 1]).astype(bf16)
        found = jnp.dot(query_in, w_query[side], preferred_element_type=f32).astype(bf16)
        for p in range(pairs):
            query[2 * p + side, c * rows : (c + 1) * rows] = found[p * rows : (p + 1) * rows]
        memory_in = (level * gains[1, 1 - side : 2 - side]).astype(bf16)
        found = jnp.dot(memory_in, w_keyval[1 - side], preferred_element_type=f32).astype(bf16)
        for p in range(pairs):
            keyval[2 * p + 1 - side, c * rows : (c + 1) * rows] = found[p * rows : (p + 1) * rows]


def attend(i, sides, w_out, w_head, gains, query, keyval, context, ordered, out):
    chunks, count, rows, width = sides.shape
    tokv = chunks * rows
    size = width // HEADS
    scale = 1.4426950408889634 / size**0.5
    f32, bf16 = jnp.float32, jnp.bfloat16
    side = lax.rem(i, 2)
    lane = lax.broadcasted_iota(jnp.int32, (tokv, 2 * size), 1)
    first = lane < size
    zero = jnp.zeros((tokv, 2 * size), bf16)
    ones = jnp.ones((tokv, 2 * size), bf16)
    counts = jnp.concatenate([jnp.where(first, ones, zero), jnp.where(first, zero, ones)], axis=0)

    def stack(columns):
        both = keyval[i, :, columns]
        return jnp.concatenate([jnp.where(first, both, zero), jnp.where(first, zero, both)], axis=0)

    def score(h):
        columns = slice(h * size, (h + 2) * size)
        return lax.dot_general(
            query[i, :, columns], stack(columns), (((1,), (1,)), ((), ())), preferred_element_type=f32
        )

    ahead = score(0)
    for h in range(0, HEADS, 2):
        scores = ahead
        if h + 2 < HEADS:
            ahead = score(h + 2)
        probs = []
        for half in range(2):
            own = scores[:, half * tokv : (half + 1) * tokv]
            top = jnp.max(own, axis=-1, keepdims=True)
            probs.append(jnp.exp2((own - top) * scale).astype(bf16))
        values = stack(slice(width + h * size, width + (h + 2) * size))
        total = jnp.dot(
            jnp.concatenate(probs, axis=1),
            jnp.concatenate([values, counts], axis=1),
            preferred_element_type=f32,
        )
        context[:, h * size : (h + 2) * size] = (total[:, : 2 * size] / total[:, 2 * size :]).astype(bf16)
    emb = jnp.concatenate([sides[c, i] for c in range(chunks)], axis=0)
    updated = emb.astype(f32) + jnp.dot(context[...], w_out[side], preferred_element_type=f32)
    final = (normal(updated) * gains[2, pl.ds(side, 1)]).astype(bf16)
    parts = rows // ROWS
    for c in range(chunks):
        for j in range(parts):
            place = (j * chunks + c) * ROWS
            come = (c * parts + j) * ROWS
            ordered[place : place + ROWS] = final[come : come + ROWS]
    head = lax.dot_general(
        w_head[side], ordered[...], (((1,), (1,)), ((), ())), preferred_element_type=f32
    )
    conf = 1.0 + jnp.exp(head[3:4])
    for c in range(4):
        record = conf * head[c : c + 1] if c < 3 else conf
        for b in range(tokv // 128):
            row = c * (tokv // 128) + b
            out[row // 2, pl.ds(row % 2 * count + i, 1), :] = record[:, b * 128 : (b + 1) * 128]


def plan(nz, count, view_dev, z, y, pairs, wanted, keys, places):
    total = 2 * pairs.shape[1]
    shape = wanted.shape
    lane = lax.broadcasted_iota(jnp.int32, shape, 1)
    views = [pairs[k % 2, k // 2] for k in range(total)]
    bits = view_dev.bit_length() - 1
    owners = [lax.shift_right_logical(v, bits) for v in views]
    asks = jnp.zeros(shape, jnp.int32)
    labels = jnp.zeros(shape, jnp.int32)
    for k in range(total):
        rank = jnp.int32(0)
        for j in range(k):
            rank = jnp.where(owners[j] == owners[k], 1, rank)
        asks = jnp.where(lane == owners[k] * 2 + rank, views[k] & (view_dev - 1), asks)
        for sub in range(2):
            spot = k // count * 2 * count + sub * count + k % count
            labels = jnp.where(lane == spot, views[k] * 2 + sub, labels)
        d = (lax.shift_right_logical(owners[k], NY.bit_length() - 1) - z + nz) & (nz - 1)
        come = (owners[k] - y + NY) & (NY - 1)
        base = jnp.where(come == 0, 3, jnp.where(come == NY - 1, 0, come))
        spot = jnp.where(d == 0, 0, jnp.where(2 * d < nz, 2 * d, 2 * (nz - d) - 1))
        places[k] = base * (2 * nz) + 2 * spot + rank
    wanted[...] = asks
    keys[...] = labels


def kernel(nz, nm, chunks, *refs):
    refs = iter(refs)

    def take(n):
        return [next(refs) for unused in range(n)]

    tokens, pairs, w_head, gains = take(4)
    in_hbm = take(4)
    (sums,) = take(1)
    w_embed, w_query, w_keyval, w_out = in_vmem = take(4)
    wanted, keys, places, full, w_near, w_held, slots, parcels, sides = take(9)
    query, keyval, context, ordered, out, block, toward, came, half, came_y, mine_sum, every = take(12)
    pools = take(chunks)
    held = [take(nz) for unused in range(chunks)]
    (local, s1, r1, s2, r2, s4, r4, s3, r3, t_send, t_recv, w_send, w_recv) = take(13)
    (z_send, z_recv, p_send, p_recv, y_send, y_recv, x_send, x_recv) = take(8)

    view = lax.axis_index("view")
    me = lax.axis_index("mp")
    z = view // NY
    y = view % NY
    nv = nz * NY
    part = tokens.shape[1] // nm
    feat = tokens.shape[2]
    view_dev = tokens.shape[0]
    total = 2 * pairs.shape[1]
    count = total // nm
    tokv = tokens.shape[1]

    def at_z(step):
        return (lax.rem(z + step + nz, nz) * NY + y, me)

    def at_y(step):
        return (z * NY + lax.rem(y + step + NY, NY), me)

    column_peers = [(view, lax.rem(me + o, nm)) for o in range(1, nm)]
    peers = column_peers + [at_z(o) for o in range(1, nz)] + [at_y(o) for o in range(1, NY)]
    barrier = pltpu.get_barrier_semaphore()
    for peer in peers:
        pl.semaphore_signal(barrier, inc=1, device_id=peer, device_id_type=MESH)
    loads = [pltpu.make_async_copy(a, b, local.at[k]) for k, (a, b) in enumerate(zip(in_hbm, in_vmem))]
    loads[0].start()
    own = pltpu.make_async_copy(
        tokens.at[:, pl.ds(pl.multiple_of(me * part, ROWS), part), :],
        full.at[:, :, pl.ds(pl.multiple_of(me * feat, 128), feat)],
        local.at[4],
    )
    own.start()
    plan(nz, count, view_dev, z, y, pairs, wanted, keys, places)
    w_near[0] = wanted[...]
    pl.semaphore_wait(barrier, len(peers))

    sent = []

    def start(copy):
        copy.start()
        sent.append(copy)
        return copy

    def finish(keep=0):
        for copy in sent[: len(sent) - keep]:
            copy.wait_send()
        del sent[: len(sent) - keep]

    def receive(copies):
        for copy in copies:
            copy.wait_recv()

    arriving = []
    for o in range(1, nm):
        j = lax.rem(me + o, nm)
        arriving.append(
            start(
                remote(
                    tokens.at[:, pl.ds(pl.multiple_of(j * part, ROWS), part), :],
                    full.at[:, :, pl.ds(pl.multiple_of(me * feat, 128), feat)],
                    t_send.at[o],
                    t_recv.at[o],
                    column_peers[o - 1],
                )
            )
        )
    asking = [
        start(remote(wanted, w_near.at[NY - o], w_send.at[o], w_recv.at[NY - o], at_y(o)))
        for o in range(1, NY)
    ]
    for load in loads[1:]:
        load.start()
    own.wait()
    loads[0].wait()
    receive(arriving)
    emb = jnp.dot(
        full[...].reshape(view_dev * part, nm * feat), w_embed[...], preferred_element_type=jnp.float32
    )
    emb = emb.astype(jnp.bfloat16).reshape(view_dev, part, -1)
    for c in range(chunks):
        held[c][0][0:view_dev] = emb[:, c * ROWS : (c + 1) * ROWS]

    z_copy, y_copy, x_copy = {}, {}, {}
    p_copy = {
        c: start(
            remote(
                held[c][0].at[pl.ds(0, view_dev)],
                held[c][0].at[pl.ds(view_dev, view_dev)],
                p_send.at[c],
                p_recv.at[c],
                at_y(2),
            )
        )
        for c in range(chunks)
        if FAR[c]
    }
    first_slot = [lax.rem(z + d, nz) * (NY * 2) for d in range(nz)]
    column_slot = [lax.rem(y + dy, NY) * 2 for dy in range(NY)]

    def choose(c, d, column, dest, r):
        local = w_held[dest, 0, first_slot[d] + column_slot[column] + r]
        return held[c][d][local if column == 0 else local + view_dev]

    def near(c, t):
        if t == 0 and FAR[c]:
            p_copy[c].wait_recv()
        for d, ways in offsets(nz, c, t):
            if t:
                z_copy[c, d].wait_recv()
            for way in ways:
                target = (d - way) % nz
                z_copy[c, target] = start(
                    remote(
                        held[c][d],
                        held[c][target],
                        z_send.at[c, target],
                        z_recv.at[c, target],
                        at_z(way),
                    )
                )

    def send_slots(c, t):
        found = [d for d, unused in offsets(nz, c, t)]
        low = 2 * min(position(nz, d) for d in found)
        for way, dest in enumerate((1, 3) if FAR[c] else (1, 3, 2)):
            for d in found:
                for r in range(2):
                    slots[c, way, 2 * position(nz, d) + r] = choose(c, d, 0, dest, r)
            y_copy[c, way, t] = start(
                remote(
                    slots.at[c, way, pl.ds(low, 2 * len(found))],
                    pools[c].at[pl.ds(2 * nz * way + low, 2 * len(found))],
                    y_send.at[c, way, t],
                    y_recv.at[c, way, t],
                    at_y(dest),
                )
            )
        for d in found:
            for r in range(2):
                pools[c][6 * nz + 2 * position(nz, d) + r] = choose(c, d, 0, 0, r)
                if FAR[c]:
                    pools[c][4 * nz + 2 * position(nz, d) + r] = choose(c, d, 2, 0, r)

    def hand(c, unused):
        receive([copy for key, copy in y_copy.items() if key[0] == c])
        rows = pl.ds(pl.multiple_of(me * ROWS, ROWS), ROWS)
        for o in range(1, nm):
            j = lax.rem(me + o, nm)
            for k in range(count):
                parcels[c, o, k] = pools[c][places[j * count + k]]
            x_copy[c, o] = start(
                remote(
                    parcels.at[c, o],
                    sides.at[c, :, rows, :],
                    x_send.at[c, o],
                    x_recv.at[c, o],
                    column_peers[o - 1],
                )
            )
        for k in range(count):
            sides[c, k, rows, :] = pools[c][places[me * count + k]]

    acts = (near, send_slots, hand)
    asked = False
    for kind, c, t in ORDER:
        if not asked and kind == 1:
            asked = True
            receive(asking)
            to_scalars = pltpu.make_async_copy(w_near, w_held, local.at[6])
            to_scalars.start()
            to_scalars.wait()
        acts[kind](c, t)
    for load in loads[1:]:
        load.wait()
    finish(keep=nm - 1)
    for c in range(chunks):
        receive([x_copy[c, o] for o in range(1, nm)])
        project(c, sides, w_query, w_keyval, gains, query, keyval)

    @pl.loop(0, count)
    def one_side(i):
        attend(i, sides, w_out, w_head, gains, query, keyval, context, ordered, out)

    receive(
        [
            start(remote(out.at[lax.rem(me + o, nm)], block.at[me], s1.at[o], r1.at[o], column_peers[o - 1]))
            for o in range(1, nm)
        ]
    )
    block[me] = out[me]
    row = lax.broadcasted_iota(jnp.int32, (nv * 8, nm * 8), 0)
    toward[...] = jnp.dot(
        jnp.where(row == keys[0:1, 0 : nm * 8], 1.0, 0.0),
        block[...].reshape(nm * 8, 128),
        precision=lax.Precision.HIGHEST,
        preferred_element_type=jnp.float32,
    ).reshape(nv, 8, 128)
    came[z] = toward[pl.ds(z * NY, NY)]
    receive(
        [
            start(
                remote(
                    toward.at[pl.ds(lax.rem(z + o, nz) * NY, NY)], came.at[z], s2.at[o], r2.at[o], at_z(o)
                )
            )
            for o in range(1, nz)
        ]
    )
    half[...] = jnp.sum(came[...], axis=0)
    came_y[y] = half[y]
    receive(
        [
            start(remote(half.at[lax.rem(y + o, NY)], came_y.at[y], s4.at[o], r4.at[o], at_y(o)))
            for o in range(1, NY)
        ]
    )
    mine_sum[...] = jnp.sum(came_y[...], axis=0)
    every[me] = mine_sum[...]
    receive(
        [
            start(remote(mine_sum, every.at[me], s3.at[o], r3.at[o], column_peers[o - 1]))
            for o in range(1, nm)
        ]
    )
    blocks = tokv // 128
    for index in range(view_dev):
        for row in range(4 * blocks):
            place = row % blocks * 128
            sums[index, row // blocks, place : place + 128] = every[row // 2, index * 2 + row % 2]
    finish()


def on_device(tokens, pairs, w_embed, w_query, w_keyval, w_out, w_head, gains):
    nv = lax.axis_size("view")
    nm = lax.axis_size("mp")
    nz = nv // NY
    view_dev, tokv, feat = tokens.shape
    width = w_embed.shape[1]
    count = 2 * pairs.shape[0] // nm
    ask = (8, 128)
    part = tokv // nm
    chunks = part // ROWS
    piece = (ROWS, width)
    f32, bf16, i32 = jnp.float32, jnp.bfloat16, jnp.int32
    vmem = pl.BlockSpec(memory_space=pltpu.VMEM)
    hbm = pl.BlockSpec(memory_space=pltpu.HBM)
    dma = pltpu.SemaphoreType.DMA
    weights = (w_embed, w_query, w_keyval, w_out)
    return pl.pallas_call(
        functools.partial(kernel, nz, nm, chunks),
        out_shape=jax.ShapeDtypeStruct((view_dev, 4, tokv), f32),
        in_specs=[hbm, pl.BlockSpec(memory_space=pltpu.SMEM), vmem, vmem] + [hbm] * 4,
        out_specs=vmem,
        scratch_shapes=[pltpu.VMEM(w.shape, bf16) for w in weights]
        + [
            pltpu.VMEM(ask, i32),
            pltpu.VMEM(ask, i32),
            pltpu.SMEM((2 * pairs.shape[0],), i32),
            pltpu.VMEM((view_dev, part, nm * feat), bf16),
            pltpu.VMEM((NY,) + ask, i32),
            pltpu.SMEM((NY,) + ask, i32),
            pltpu.VMEM((chunks, 3, 2 * nz) + piece, bf16),
            pltpu.VMEM((chunks, nm, count) + piece, bf16),
            pltpu.VMEM((chunks, count, nm * ROWS, width), bf16),
            pltpu.VMEM((count, tokv, width), bf16),
            pltpu.VMEM((count, tokv, 2 * width), bf16),
            pltpu.VMEM((tokv, width), bf16),
            pltpu.VMEM((tokv, width), bf16),
            pltpu.VMEM((nm, 8, 128), f32),
            pltpu.VMEM((nm, 8, 128), f32),
            pltpu.VMEM((nv, 8, 128), f32),
            pltpu.VMEM((nz, NY, 8, 128), f32),
            pltpu.VMEM((NY, 8, 128), f32),
            pltpu.VMEM((NY, 8, 128), f32),
            pltpu.VMEM((8, 128), f32),
            pltpu.VMEM((nm, 8, 128), f32),
        ]
        + [pltpu.VMEM((8 * nz,) + piece, bf16)] * chunks
        + [
            pltpu.VMEM(((2 if FAR[c] else 1) * view_dev,) + piece, bf16)
            for c in range(chunks)
            for unused in range(nz)
        ]
        + [dma((7,))]
        + [dma((nm,))] * 2
        + [dma((nz,))] * 2
        + [dma((NY,))] * 2
        + [dma((nm,))] * 4
        + [dma((NY,))] * 2
        + [dma((chunks, nz))] * 2
        + [dma((chunks,))] * 2
        + [dma((chunks, 3, nz // 2 + 1))] * 2
        + [dma((chunks, nm))] * 2,
        compiler_params=pltpu.CompilerParams(
            collective_id=0, has_side_effects=True, vmem_limit_bytes=60 * 2**20
        ),
    )(tokens, pairs.T, w_head, jnp.transpose(gains, (1, 0, 2)), *weights)


def solution(mesh):
    return jax.shard_map(
        on_device,
        mesh=mesh,
        in_specs=(P("view", None, "mp"), P("view", None), P(), P(), P(), P(), P(), P()),
        out_specs=P("view", None, None),
        check_vma=False,
    )
```

time: 123 us -> 113 us (0.919)
  Pallas kernels: 116 us -> 112 us
  local copies, waits for them, and re-layouts: 4.29 us -> 1.35 us
  other arithmetic: 1.63 us -> 0 us
    pallas_call x1, Pallas kernels: 116 us -> 112 us  [on_device(): pl.pallas_call(functools.partial(kernel, nz, nm, chunks), out_shape=jax.S...]
    unnamed x3 -> x1, local copies, waits for them, and re-layouts: 3.45 us -> 1.35 us
where the time goes in v5:
time: 113 us
  Pallas kernels  112 us (99%)
  local copies, waits for them, and re-layouts  1.35 us (1%)
    pallas_call x1, Pallas kernels, on_device(): pl.pallas_call(functools.partial(kernel, nz, nm, chunks), out_shape=jax.S...  112 us

profile of v5, /device:TPU:1, one launch (start us, length us, event | category | flops | bytes accessed | tf_op | source)
XLA Modules:
  0.0 113.0 jit_solution(2304278300930688512)
XLA Ops:
  0.0 111.6 %shard_map.82 = f32[4,4,384]{2,1,0:T(4,128)} custom-call(bf16[4,384,128]{2,1,0:T(8,128)(2,1)} %refs_0_.1, s32[2,16]{1,0:T(2,128)} %bitcast.3, bf16[2,4,768]{2,1,0:T(4,128)(2,1)} %refs_2_.1, f32[3,2,768]{2,1,0:T(2,128)} %bitcast.2, bf16[1024,768]{1,0:T(8,128)(2,1)} %refs_4_.1, bf16[2,768,768]{2,1,0:T(8,128)(2,1)} %refs_5_.1, bf16[2,768,1536]{2,1,0:T(8,128)(2,1)} %refs_6_.1, ...), custom_call_target="tpu_custom_call" | custom-call | tf_op jit(solution)/shard_map/pallas_call | solution.py:454
  111.6 1.3 %copy.10 = f32[4,4,384]{2,1,0:T(4,128)} copy(f32[4,4,384]{2,1,0:T(4,128)} %shard_map.82) | data formatting | bytes 49152

commit v6 on v5

--- a/solution.py
+++ b/solution.py
@@ -11,40 +11,40 @@
 NY = 4
 ROWS = 16
 MESH = pl.DeviceIdType.MESH
-FAR = (False, True, True)
+FAR = (False, False, True)
 ORDER = (
     (0, 0, 0),
+    (0, 1, 0),
+    (1, 0, 0),
     (0, 0, 1),
-    (0, 1, 0),
+    (1, 0, 1),
+    (0, 1, 1),
+    (1, 1, 1),
     (0, 0, 2),
-    (1, 0, 1),
+    (0, 1, 2),
+    (0, 0, 3),
+    (0, 2, 0),
+    (1, 0, 2),
+    (1, 0, 3),
+    (0, 1, 3),
+    (0, 2, 1),
+    (0, 0, 4),
+    (1, 0, 4),
     (1, 1, 0),
-    (0, 1, 1),
-    (0, 0, 3),
-    (1, 0, 0),
-    (1, 0, 2),
-    (0, 1, 2),
-    (1, 0, 3),
-    (0, 0, 4),
-    (0, 2, 0),
-    (1, 0, 4),
-    (0, 1, 3),
     (1, 1, 2),
-    (1, 2, 0),
-    (0, 2, 1),
+    (0, 1, 4),
+    (0, 2, 2),
+    (2, 0, 0),
+    (1, 1, 4),
     (1, 1, 3),
-    (2, 0, 0),
-    (1, 1, 1),
-    (0, 1, 4),
-    (1, 1, 4),
-    (1, 2, 1),
-    (0, 2, 2),
+    (0, 2, 3),
     (1, 2, 2),
-    (2, 1, 0),
-    (0, 2, 3),
     (1, 2, 3),
     (0, 2, 4),
     (1, 2, 4),
+    (2, 1, 0),
+    (1, 2, 1),
+    (1, 2, 0),
     (2, 2, 0),
 )
 

time: 113 us -> 112 us (level)
  Pallas kernels: 112 us -> 110 us
    pallas_call x1, Pallas kernels: 112 us -> 110 us  [on_device(): pl.pallas_call(functools.partial(kernel, nz, nm, chunks), out_shape=jax.S...]
where the time goes in v6:
time: 112 us
  Pallas kernels  110 us (98%)
  local copies, waits for them, and re-layouts  1.35 us (1%)
    pallas_call x1, Pallas kernels, on_device(): pl.pallas_call(functools.partial(kernel, nz, nm, chunks), out_shape=jax.S...  110 us

profile of v6, /device:TPU:1, one launch (start us, length us, event | category | flops | bytes accessed | tf_op | source)
XLA Modules:
  0.0 111.6 jit_solution(15879035331958250698)
XLA Ops:
  0.0 110.2 %shard_map.82 = f32[4,4,384]{2,1,0:T(4,128)} custom-call(bf16[4,384,128]{2,1,0:T(8,128)(2,1)} %refs_0_.1, s32[2,16]{1,0:T(2,128)} %bitcast.3, bf16[2,4,768]{2,1,0:T(4,128)(2,1)} %refs_2_.1, f32[3,2,768]{2,1,0:T(2,128)} %bitcast.2, bf16[1024,768]{1,0:T(8,128)(2,1)} %refs_4_.1, bf16[2,768,768]{2,1,0:T(8,128)(2,1)} %refs_5_.1, bf16[2,768,1536]{2,1,0:T(8,128)(2,1)} %refs_6_.1, ...), custom_call_target="tpu_custom_call" | custom-call | tf_op jit(solution)/shard_map/pallas_call | solution.py:454
  110.2 1.3 %copy.10 = f32[4,4,384]{2,1,0:T(4,128)} copy(f32[4,4,384]{2,1,0:T(4,128)} %shard_map.82) | data formatting | bytes 49152

commit v7 on v6

--- a/solution.py
+++ b/solution.py
@@ -273,8 +273,6 @@
         start(remote(wanted, w_near.at[NY - o], w_send.at[o], w_recv.at[NY - o], at_y(o)))
         for o in range(1, NY)
     ]
-    for load in loads[1:]:
-        load.start()
     own.wait()
     loads[0].wait()
     receive(arriving)
@@ -374,6 +372,8 @@
             to_scalars = pltpu.make_async_copy(w_near, w_held, local.at[6])
             to_scalars.start()
             to_scalars.wait()
+            for load in loads[1:]:
+                load.start()
         acts[kind](c, t)
     for load in loads[1:]:
         load.wait()

time: 112 us -> 112 us (level)
  no operation moved by 1% of the time
where the time goes in v7:
time: 112 us
  Pallas kernels  110 us (98%)
  local copies, waits for them, and re-layouts  1.35 us (1%)
    pallas_call x1, Pallas kernels, on_device(): pl.pallas_call(functools.partial(kernel, nz, nm, chunks), out_shape=jax.S...  110 us

profile of v7, /device:TPU:1, one launch (start us, length us, event | category | flops | bytes accessed | tf_op | source)
XLA Modules:
  0.0 111.6 jit_solution(17773791795496889483)
XLA Ops:
  0.0 110.2 %shard_map.82 = f32[4,4,384]{2,1,0:T(4,128)} custom-call(bf16[4,384,128]{2,1,0:T(8,128)(2,1)} %refs_0_.1, s32[2,16]{1,0:T(2,128)} %bitcast.3, bf16[2,4,768]{2,1,0:T(4,128)(2,1)} %refs_2_.1, f32[3,2,768]{2,1,0:T(2,128)} %bitcast.2, bf16[1024,768]{1,0:T(8,128)(2,1)} %refs_4_.1, bf16[2,768,768]{2,1,0:T(8,128)(2,1)} %refs_5_.1, bf16[2,768,1536]{2,1,0:T(8,128)(2,1)} %refs_6_.1, ...), custom_call_target="tpu_custom_call" | custom-call | tf_op jit(solution)/shard_map/pallas_call | solution.py:454
  110.2 1.3 %copy.10 = f32[4,4,384]{2,1,0:T(4,128)} copy(f32[4,4,384]{2,1,0:T(4,128)} %shard_map.82) | data formatting | bytes 49152
